TPU v7x, 256 devices: a whole 4x4x8 slice. The times are simulated.
256 devices in a mesh: dp: 8 (over x, z_hi), ctx: 32 (over y, z_lo, core).
Axes of the slice: x: 4, y: 4, z: 8 (z_hi: 2, z_lo: 4; z = z_hi * 4 + z_lo), core: 2. Of those that a mesh axis runs over, the one named last changes fastest.
Arguments:
- signal: bfloat16 [8, 128, 32768], P('dp', None, 'ctx'), may hold values from -6 to 6
- gate: bfloat16 [8, 128, 32768], P('dp', None, 'ctx'), may hold values from -6 to 6
- filter_param: bfloat16 [128, 32768], P(None, 'ctx'), may hold values from -6 to 6
- cotangent: bfloat16 [8, 128, 32768], P('dp', None, 'ctx'), may hold values from -6 to 6
Outputs:
- gated: bfloat16 [8, 128, 32768], P('dp', None, 'ctx')
- grad_signal: bfloat16 [8, 128, 32768], P('dp', None, 'ctx')
- grad_gate: bfloat16 [8, 128, 32768], P('dp', None, 'ctx')
- grad_filter: bfloat16 [128, 32768], P('dp', 'ctx')
All inputs are finite; a program needn't handle non-finite values.
Results may differ from a plain program's by a relative error of at most 0.019.
Values may be sent and summed in bfloat16 or wider, within the bound.
A program may use at most 128 MiB of HBM per device.

v0:
```python
import math

import jax
import jax.numpy as jnp
from jax import lax
from jax.sharding import PartitionSpec as P

N1 = 1024


def angle_table(row_ids, col_ids, modulus):
    product = row_ids[:, None] * col_ids[None, :] % modulus
    return 2.0 * math.pi / modulus * product.astype(jnp.float32)


def fourier_pair(row_ids, col_ids, modulus):
    angles = angle_table(row_ids, col_ids, modulus)
    return (jnp.cos(angles).astype(jnp.bfloat16), jnp.sin(angles).astype(jnp.bfloat16))


def twiddle_pair(row_ids, col_ids, modulus):
    angles = angle_table(row_ids, col_ids, modulus)
    return (jnp.cos(angles), jnp.sin(angles))


def per_device(signal, gate, filter_param, cotangent):
    ctx_size = lax.axis_size("ctx")
    dp_size = lax.axis_size("dp")
    place = lax.axis_index("ctx")
    channels = signal.shape[1]
    length = signal.shape[2]
    rows_dev = length // N1
    cols_dev = N1 // ctx_size
    length_two = 2 * rows_dev * ctx_size
    freq_dev = length_two // ctx_size
    half_two = length_two // 2
    full_length = length_two * N1
    filt_scale = (full_length // 2) ** (-0.5)
    own_share = channels // dp_size
    every_one = jnp.arange(N1, dtype=jnp.int32)
    every_two = jnp.arange(length_two, dtype=jnp.int32)
    cos_one, sin_one = fourier_pair(every_one, every_one, N1)
    cos_two, sin_two = fourier_pair(every_two[:half_two], every_two, length_two)
    my_cols = place * cols_dev + jnp.arange(cols_dev, dtype=jnp.int32)
    my_freq = place * freq_dev + jnp.arange(freq_dev, dtype=jnp.int32)
    turn_cos_a, turn_sin_a = twiddle_pair(my_cols, every_two, full_length)
    turn_cos_b, turn_sin_b = twiddle_pair(every_one, my_freq, full_length)
    back_cos = cos_two.reshape(half_two, ctx_size, freq_dev)
    back_sin = sin_two.reshape(half_two, ctx_size, freq_dev)

    def section_rows(pieces):
        number = pieces.shape[0]
        real_a = jnp.einsum("mpq,pk->mqk", pieces, cos_two, preferred_element_type=jnp.float32)
        imag_a = -jnp.einsum("mpq,pk->mqk", pieces, sin_two, preferred_element_type=jnp.float32)
        real_b = (real_a * turn_cos_a + imag_a * turn_sin_a).astype(jnp.bfloat16)
        imag_b = (imag_a * turn_cos_a - real_a * turn_sin_a).astype(jnp.bfloat16)

        def regroup(member):
            return (
                member.reshape(number, cols_dev, ctx_size, freq_dev)
                .transpose(0, 2, 1, 3)
                .reshape(number, ctx_size, cols_dev * freq_dev)
            )

        return (regroup(real_b), regroup(imag_b))

    def section_cols(pieces):
        number = pieces[0].shape[0]
        real_q = pieces[0].reshape(number, N1, freq_dev)
        imag_q = pieces[1].reshape(number, N1, freq_dev)

        def apply_table(member, matrix):
            return jnp.einsum("mqk,ql->mkl", member, matrix, preferred_element_type=jnp.float32)

        real_f = apply_table(real_q, cos_one) + apply_table(imag_q, sin_one)
        imag_f = apply_table(imag_q, cos_one) - apply_table(real_q, sin_one)
        return (real_f, imag_f)

    def section_back(pieces):
        number = pieces[0].shape[0]
        real_q = pieces[0].reshape(number, ctx_size, cols_dev, freq_dev)
        imag_q = pieces[1].reshape(number, ctx_size, cols_dev, freq_dev)
        values = jnp.einsum(
            "mjqk,pjk->mqp", real_q, back_cos, preferred_element_type=jnp.float32
        ) - jnp.einsum("mjqk,pjk->mqp", imag_q, back_sin, preferred_element_type=jnp.float32)
        return values * (1.0 / full_length)

    def forward(signals):
        number = signals.shape[0]
        outgoing = (
            signals.reshape(number, rows_dev, ctx_size, cols_dev)
            .transpose(0, 2, 1, 3)
            .reshape(number, ctx_size, rows_dev * cols_dev)
        )
        halves = section_rows(
            lax.all_to_all(outgoing, "ctx", split_axis=1, concat_axis=1, tiled=True)
        )
        return section_cols(
            (
                lax.all_to_all(halves[0], "ctx", split_axis=1, concat_axis=1, tiled=True),
                lax.all_to_all(halves[1], "ctx", split_axis=1, concat_axis=1, tiled=True),
            )
        )

    def inverse(spectra, factors):
        number = spectra[0].shape[0]
        real_e = spectra[0].astype(jnp.bfloat16)
        imag_e = spectra[1].astype(jnp.bfloat16)

        def apply_table(member, matrix):
            return jnp.einsum("mkl,ql->mqk", member, matrix, preferred_element_type=jnp.float32)

        real_b = apply_table(real_e, cos_one) - apply_table(imag_e, sin_one)
        imag_b = apply_table(real_e, sin_one) + apply_table(imag_e, cos_one)
        real_c = (
            (real_b * turn_cos_b - imag_b * turn_sin_b)
            .astype(jnp.bfloat16)
            .reshape(number, ctx_size, cols_dev * freq_dev)
        )
        imag_c = (
            (real_b * turn_sin_b + imag_b * turn_cos_b)
            .astype(jnp.bfloat16)
            .reshape(number, ctx_size, cols_dev * freq_dev)
        )
        values = section_back(
            (
                lax.all_to_all(real_c, "ctx", split_axis=1, concat_axis=1, tiled=True),
                lax.all_to_all(imag_c, "ctx", split_axis=1, concat_axis=1, tiled=True),
            )
        )
        scaled = (values * factors[:, None, None]).astype(jnp.bfloat16)
        outgoing = (
            scaled.reshape(number, cols_dev, ctx_size, rows_dev)
            .transpose(0, 2, 3, 1)
            .reshape(number, ctx_size, rows_dev * cols_dev)
        )
        arrived = lax.all_to_all(outgoing, "ctx", split_axis=1, concat_axis=1, tiled=True)
        return (
            arrived.reshape(number, ctx_size, rows_dev, cols_dev)
            .transpose(0, 2, 1, 3)
            .reshape(number, length)
        )

    tokens = signal.reshape(channels, length)
    gates = gate.reshape(channels, length)
    grads_in = cotangent.reshape(channels, length)
    mid_grad = (grads_in.astype(jnp.float32) * gates.astype(jnp.float32)).astype(jnp.bfloat16)
    unit = jnp.ones((channels,), jnp.float32)
    leading = forward(jnp.concatenate([tokens, filter_param], axis=0))
    spec_x = (leading[0][:channels], leading[1][:channels])
    spec_h = (leading[0][channels:] * filt_scale, leading[1][channels:] * filt_scale)
    conv = inverse(
        (
            spec_h[0] * spec_x[0] - spec_h[1] * spec_x[1],
            spec_h[0] * spec_x[1] + spec_h[1] * spec_x[0],
        ),
        unit,
    )
    spec_g = forward(mid_grad)
    reduced = (
        lax.psum((spec_x[0] * spec_g[0] + spec_x[1] * spec_g[1]).astype(jnp.bfloat16), "dp").astype(
            jnp.float32
        ),
        lax.psum((spec_x[0] * spec_g[1] - spec_x[1] * spec_g[0]).astype(jnp.bfloat16), "dp").astype(
            jnp.float32
        ),
    )
    filter_count = reduced[0].shape[0]
    stacked = (
        jnp.concatenate([spec_h[0] * spec_g[0] + spec_h[1] * spec_g[1], reduced[0]], axis=0),
        jnp.concatenate([spec_h[0] * spec_g[1] - spec_h[1] * spec_g[0], reduced[1]], axis=0),
    )
    factors = jnp.concatenate([unit, filt_scale * jnp.ones((filter_count,), jnp.float32)])
    results = inverse(stacked, factors)
    grad_signal = results[:channels]
    grad_filter = results[channels:]
    gated = (gates.astype(jnp.float32) * conv.astype(jnp.float32)).astype(jnp.bfloat16)
    grad_gate = (grads_in.astype(jnp.float32) * conv.astype(jnp.float32)).astype(jnp.bfloat16)
    return (
        gated[None],
        grad_signal[None],
        grad_gate[None],
        lax.dynamic_slice_in_dim(grad_filter, lax.axis_index("dp") * own_share, own_share, 0),
    )


def solution(mesh):
    in_specs = (P("dp", None, "ctx"), P("dp", None, "ctx"), P(None, "ctx"), P("dp", None, "ctx"))
    out_specs = (P("dp", None, "ctx"), P("dp", None, "ctx"), P("dp", None, "ctx"), P("dp", "ctx"))
    return jax.shard_map(
        per_device, mesh=mesh, in_specs=in_specs, out_specs=out_specs, check_vma=False
    )
```

profile of v0, /device:TPU:1, one launch (start us, length us, event | category | flops | bytes accessed | tf_op | source)
XLA Modules:
  0.0 612.3 jit_solution(13117150914239558221)
XLA Ops:
  10.3 10.2 %all-to-all-start.6 = ((bf16[128,32,32]{0,2,1:T(8,128)(2,1)}), bf16[128,32,32]{0,2,1:T(8,128)(2,1)S(1)}, u32[]{:S(2)}, u32[]{:S(2)}) async-start(bf16[128,32,32]{0,2,1:T(8,128)(2,1)} %bitcast.26), calls=%async_computation.6 | async-start | bytes 524288 | tf_op jit(solution)/shard_map/all_to_all | solution.py:96
  21.7 10.0 %all-to-all-done.6 = bf16[128,32,32]{0,2,1:T(8,128)(2,1)S(1)} async-done(((bf16[128,32,32]{0,2,1:T(8,128)(2,1)}), bf16[128,32,32]{0,2,1:T(8,128)(2,1)S(1)}, u32[]{:S(2)}, u32[]{:S(2)}) %all-to-all-start.6) | async-done | bytes 262176 | tf_op jit(solution)/shard_map/all_to_all | solution.py:96
  31.8 3.7 all-to-all-start
  38.4 13.9 %all-to-all-done = bf16[256,32,32]{0,2,1:T(8,128)(2,1)S(1)} async-done(((bf16[256,32,32]{0,2,1:T(8,128)(2,1)}), bf16[256,32,32]{0,2,1:T(8,128)(2,1)S(1)}, u32[]{:S(2)}, u32[]{:S(2)}) %all-to-all-start) | async-done | bytes 524320 | tf_op jit(solution)/shard_map/all_to_all | solution.py:96
  52.3 3.7 all-to-all-start.7
  57.1 15.8 %all-to-all-done.7 = bf16[128,32,64]{0,2,1:T(8,128)(2,1)S(1)} async-done(((bf16[128,32,64]{0,2,1:T(8,128)(2,1)}), bf16[128,32,64]{0,2,1:T(8,128)(2,1)S(1)}, u32[]{:S(2)}, u32[]{:S(2)}) %all-to-all-start.7) | async-done | bytes 524320 | tf_op jit(solution)/shard_map/all_to_all | solution.py:100
  72.9 3.7 all-to-all-start.8
  77.3 3.1 subtract_convert_fusion.1
  81.0 1.6 copy.55
  82.6 11.0 %all-to-all-done.8 = bf16[128,32,64]{0,2,1:T(8,128)(2,1)S(1)} async-done(((bf16[128,32,64]{0,2,1:T(8,128)(2,1)}), bf16[128,32,64]{0,2,1:T(8,128)(2,1)S(1)}, u32[]{:S(2)}, u32[]{:S(2)}) %all-to-all-start.8) | async-done | bytes 524320 | tf_op jit(solution)/shard_map/all_to_all | solution.py:101
  93.5 3.7 all-to-all-start.2
  97.5 1.5 reshape.267
  99.2 1.6 copy.52
  101.9 23.4 %all-to-all-done.2 = bf16[256,32,64]{0,2,1:T(8,128)(2,1)S(1)} async-done(((bf16[256,32,64]{0,2,1:T(8,128)(2,1)}), bf16[256,32,64]{0,2,1:T(8,128)(2,1)S(1)}, u32[]{:S(2)}, u32[]{:S(2)}) %all-to-all-start.2) | async-done | bytes 1048608 | tf_op jit(solution)/shard_map/all_to_all | solution.py:101
  125.3 3.9 all-to-all-start.1
  129.4 17.0 %fusion.12 = f32[128,2,1024]{2,0,1:T(8,128)} fusion(bf16[128,1024,2]{1,0,2:T(8,128)(2,1)S(1)} %copy-done.4), kind=kOutput, calls=%fused_computation.19 | convolution fusion | flops 552599552 | bytes 1572864 | tf_op jit(solution)/shard_map/mqk,ql->mkl/dot_general | solution.py:73
  146.8 17.0 %fusion.14 = f32[128,2,1024]{2,0,1:T(8,128)} fusion(bf16[128,1024,2]{1,0,2:T(8,128)(2,1)S(1)} %copy.72), kind=kOutput, calls=%fused_computation.20 | convolution fusion | flops 552599552 | bytes 1572864 | tf_op jit(solution)/shard_map/mqk,ql->mkl/dot_general | solution.py:73
  163.8 17.1 %fusion.61 = f32[128,2,1024]{2,0,1:T(8,128)} fusion(f32[128,2,1024]{2,0,1:T(8,128)S(1)} %copy-done.14, bf16[128,1024,2]{1,0,2:T(8,128)(2,1)S(1)} %copy.72), kind=kOutput, calls=%fused_computation.43 | convolution fusion | flops 552861696 | bytes 2621440 | tf_op jit(solution)/shard_map/mqk,ql->mkl/dot_general | solution.py:73
  181.3 1.5 copy.56
  182.8 17.3 %fusion.22 = f32[256,2,1024]{2,0,1:T(8,128)} fusion(bf16[256,1024,2]{1,0,2:T(8,128)(2,1)S(1)} %copy.56), kind=kOutput, calls=%fused_computation.24 | convolution fusion | flops 1089470464 | bytes 3145728 | tf_op jit(solution)/shard_map/mqk,ql->mkl/dot_general | solution.py:73
  200.5 1.5 copy.53
  202.0 17.1 %fusion.20 = f32[256,2,1024]{2,0,1:T(8,128)S(1)} fusion(bf16[256,1024,2]{1,0,2:T(8,128)(2,1)S(1)} %copy.53), kind=kOutput, calls=%fused_computation.23 | convolution fusion | flops 1089470464 | bytes 3145728 | tf_op jit(solution)/shard_map/mqk,ql->mkl/dot_general | solution.py:73
  219.1 16.6 %fusion.40 = f32[256,2,1024]{2,0,1:T(8,128)S(1)} fusion(f32[256,2,1024]{2,0,1:T(8,128)S(1)} %copy-done.11, bf16[256,1024,2]{1,0,2:T(8,128)(2,1)S(1)} %copy.53), kind=kOutput, calls=%fused_computation.33 | convolution fusion | flops 1089994752 | bytes 5242880 | tf_op jit(solution)/shard_map/mqk,ql->mkl/dot_general | solution.py:73
  235.8 16.6 %fusion.43 = f32[256,2,1024]{2,0,1:T(8,128)S(1)} fusion(f32[256,2,1024]{2,0,1:T(8,128)S(1)} %fusion.20, bf16[256,1024,2]{1,0,2:T(8,128)(2,1)S(1)} %copy-done.3), kind=kOutput, calls=%fused_computation.34 | convolution fusion | flops 1089994752 | bytes 5242880 | tf_op jit(solution)/shard_map/mqk,ql->mkl/dot_general | solution.py:73
  252.5 18.6 %subtract_convert_fusion.3 = (bf16[128,2,1024]{2,0,1:T(8,128)(2,1)}, bf16[128,2,1024]{2,0,1:T(8,128)(2,1)}, bf16[128,2,1024]{2,0,1:T(8,128)(2,1)}, bf16[128,2,10...) fusion(f32[128,2,1024]{2,0,1:T(8,128)S(1)} %copy-done.13, ...), kind=kOutput, calls=%fused_computation.61 | convolution fusion | flops 559677440 | bytes 9961472 | tf_op jit(solution)/shard_map/mqk,ql->mkl/dot_general | solution.py:73
  271.1 16.0 %fusion.18 = f32[1024,128,2]{1,0,2:T(8,128)S(1)} fusion(bf16[128,2,1024]{2,0,1:T(8,128)(2,1)S(1)} %get-tuple-element.22), kind=kOutput, calls=%fused_computation.22 | convolution fusion | flops 552599552 | bytes 1572864 | tf_op jit(solution)/shard_map/mkl,ql->mqk/dot_general | solution.py:111
  287.1 16.1 %fusion.52 = f32[1024,128,2]{1,0,2:T(8,128)S(1)} fusion(f32[1024,128,2]{1,0,2:T(8,128)S(1)} %fusion.18, bf16[128,2,1024]{2,0,1:T(8,128)(2,1)S(1)} %get-tuple-element.23), kind=kOutput, calls=%fused_computation.40 | convolution fusion | flops 552861696 | bytes 2621440 | tf_op jit(solution)/shard_map/mkl,ql->mqk/dot_general | solution.py:111
  303.2 17.6 %fusion.16 = f32[1024,128,2]{1,0,2:T(8,128)S(1)} fusion(bf16[128,2,1024]{2,0,1:T(8,128)(2,1)S(1)} %get-tuple-element.23), kind=kOutput, calls=%fused_computation.21 | convolution fusion | flops 552599552 | bytes 1572864 | tf_op jit(solution)/shard_map/mkl,ql->mqk/dot_general | solution.py:111
  320.8 16.0 %fusion.77 = (bf16[128,1024,2]{0,1,2:T(8,128)(2,1)S(1)}, bf16[128,1024,2]{0,1,2:T(8,128)(2,1)S(1)}) fusion(f32[1024,128,2]{1,0,2:T(8,128)S(1)} %fusion.52, f32[1024,2]{0,1:T(2,128)S(1)} %get-tuple-element.33, f32[1024,2]{0,1:T(2,128)S(1)} %get-tuple-element.32, f32[1024,128,2]{1,0,2:T(8,128)S(1)} %fusion.16, bf16[128,2,1024]{2,0,1:T(8,128)(2,1)S(1)} %get-tuple-element.22), kind=kOutput, calls=%fused_computation.76 | convolution fusion | flops 554958848 | bytes 3686400 | tf_op jit(solution)/shard_map/mkl,ql->mqk/dot_general | solution.py:111
  336.7 1.3 copy.61
  338.1 7.8 %all-to-all-start.4 = ((bf16[128,32,64]{0,2,1:T(8,128)(2,1)}), bf16[128,32,64]{0,2,1:T(8,128)(2,1)S(1)}, u32[]{:S(2)}, u32[]{:S(2)}) async-start(bf16[128,32,64]{0,2,1:T(8,128)(2,1)} %bitcast.17), calls=%async_computation.4 | async-start | bytes 1048576 | tf_op jit(solution)/shard_map/all_to_all | solution.py:128
  345.9 1.3 copy.59
  347.2 71.0 %all-reduce.3.cloned.1.call-done = (bf16[128,2,1024]{2,0,1:T(8,128)(2,1)}, bf16[128,2,1024]{2,0,1:T(8,128)(2,1)}) async-done(((bf16[128,2,1024]{2,0,1:T(8,128)(2,1)}, bf16[128,2,1024]{2,0,1:T(8,128)(2,1)}), (bf16[128,2,1024]{2,0,1:T(8,128)(2,1)}, bf16[128,2,1024]{2,0,1:T(8,128)(2,1)})) %all-reduce.3.cloned.1.call-update) | async-done | bytes 1048592 | tf_op jit(solution)/shard_map/psum | solution.py:161
  418.3 17.1 %fusion.10 = f32[1024,256,2]{1,0,2:T(8,128)S(1)} fusion(bf16[128,2,1024]{2,0,1:T(8,128)(2,1)} %get-tuple-element.13, bf16[128,2,1024]{2,0,1:T(8,128)(2,1)S(1)} %copy-done.16), kind=kOutput, calls=%fused_computation.18 | convolution fusion | flops 1091567616 | bytes 3145728 | tf_op jit(solution)/shard_map/mkl,ql->mqk/dot_general | solution.py:111
  435.4 17.2 %fusion.46 = f32[1024,256,2]{1,0,2:T(8,128)} fusion(f32[1024,256,2]{1,0,2:T(8,128)S(1)} %fusion.10, bf16[128,2,1024]{2,0,1:T(8,128)(2,1)S(1)} %copy-done.10, bf16[128,2,1024]{2,0,1:T(8,128)(2,1)S(1)} %copy-done.17), kind=kOutput, calls=%fused_computation.35 | convolution fusion | flops 1092091904 | bytes 5242880 | tf_op jit(solution)/shard_map/mkl,ql->mqk/dot_general | solution.py:111
  452.6 11.6 %all-to-all-start.3 = ((bf16[128,32,64]{0,2,1:T(8,128)(2,1)}), bf16[128,32,64]{0,2,1:T(8,128)(2,1)S(1)}, u32[]{:S(2)}, u32[]{:S(2)}) async-start(bf16[128,32,64]{0,2,1:T(8,128)(2,1)} %bitcast.11), calls=%async_computation.3 | async-start | bytes 1048576 | tf_op jit(solution)/shard_map/all_to_all | solution.py:127
  464.3 16.0 %fusion.8 = f32[1024,256,2]{1,0,2:T(8,128)S(1)} fusion(bf16[128,2,1024]{2,0,1:T(8,128)(2,1)S(1)} %copy-done.10, bf16[128,2,1024]{2,0,1:T(8,128)(2,1)S(1)} %copy-done.17), kind=kOutput, calls=%fused_computation.17 | convolution fusion | flops 1091567616 | bytes 3145728 | tf_op jit(solution)/shard_map/mkl,ql->mqk/dot_general | solution.py:111
  480.3 17.1 %fusion.72 = (bf16[256,1024,2]{0,1,2:T(8,128)(2,1)}, bf16[256,1024,2]{0,1,2:T(8,128)(2,1)S(1)}) fusion(f32[1024,256,2]{1,0,2:T(8,128)S(1)} %copy-done.12, f32[1024,2]{0,1:T(2,128)S(1)} %get-tuple-element.33, f32[1024,2]{0,1:T(2,128)S(1)} %get-tuple-element.32, f32[1024,256,2]{1,0,2:T(8,128)S(1)} %fusion.8, bf16[128,2,1024]{2,0,1:T(8,128)(2,1)S(1)} %copy-done.9, ...), kind=kOutput, calls=%fused_computation.54 | convolution fusion | flops 1096286208 | bytes 7356416 | tf_op jit(solution)/shard_map/mkl,ql->mqk/dot_general | solution.py:111
  498.5 1.2 reshape.287
  499.7 8.0 %all-to-all-start.10 = ((bf16[256,32,64]{0,2,1:T(8,128)(2,1)}), bf16[256,32,64]{0,2,1:T(8,128)(2,1)S(1)}, u32[]{:S(2)}, u32[]{:S(2)}) async-start(bf16[256,32,64]{0,2,1:T(8,128)(2,1)} %reshape.287), calls=%async_computation.10 | async-start | bytes 2097152 | tf_op jit(solution)/shard_map/all_to_all | solution.py:128
  507.7 2.3 copy.75
  511.3 24.2 %all-to-all-done.10 = bf16[256,32,64]{0,2,1:T(8,128)(2,1)S(1)} async-done(((bf16[256,32,64]{0,2,1:T(8,128)(2,1)}), bf16[256,32,64]{0,2,1:T(8,128)(2,1)S(1)}, u32[]{:S(2)}, u32[]{:S(2)}) %all-to-all-start.10) | async-done | bytes 1048608 | tf_op jit(solution)/shard_map/all_to_all | solution.py:128
  535.5 3.9 all-to-all-start.9
  541.8 25.6 %all-to-all-done.9 = bf16[256,32,64]{0,2,1:T(8,128)(2,1)S(1)} async-done(((bf16[256,32,64]{0,2,1:T(8,128)(2,1)}), bf16[256,32,64]{0,2,1:T(8,128)(2,1)S(1)}, u32[]{:S(2)}, u32[]{:S(2)}) %all-to-all-start.9) | async-done | bytes 1048608 | tf_op jit(solution)/shard_map/all_to_all | solution.py:127
  567.4 3.9 all-to-all-start.5
  574.6 8.0 %all-to-all-done.5 = bf16[128,32,32]{0,2,1:T(8,128)(2,1)S(1)} async-done(((bf16[128,32,32]{0,2,1:T(8,128)(2,1)}), bf16[128,32,32]{0,2,1:T(8,128)(2,1)S(1)}, u32[]{:S(2)}, u32[]{:S(2)}) %all-to-all-start.5) | async-done | bytes 262176 | tf_op jit(solution)/shard_map/all_to_all | solution.py:137
  582.6 3.7 all-to-all-start.11
  588.2 15.0 %all-to-all-done.11 = bf16[256,32,32]{0,2,1:T(8,128)(2,1)S(1)} async-done(((bf16[256,32,32]{0,2,1:T(8,128)(2,1)}), bf16[256,32,32]{0,2,1:T(8,128)(2,1)S(1)}, u32[]{:S(2)}, u32[]{:S(2)}) %all-to-all-start.11) | async-done | bytes 524320 | tf_op jit(solution)/shard_map/all_to_all | solution.py:137
  (86 shorter events, 24.4 us)
Async XLA Ops:
  7.2 13.3 %copy-start.6 = (bf16[1,128,1024]{2,1,0:T(8,128)(2,1)S(1)}, bf16[1,128,1024]{2,1,0:T(8,128)(2,1)}, u32[]{:S(2)}) copy-start(bf16[1,128,1024]{2,1,0:T(8,128)(2,1)} %param.4) | copy-start | bytes 786436
  7.2 13.5 %copy-start.7 = (bf16[128,1024]{1,0:T(8,128)(2,1)S(1)}, bf16[128,1024]{1,0:T(8,128)(2,1)}, u32[]{:S(2)}) copy-start(bf16[128,1024]{1,0:T(8,128)(2,1)} %param.6) | copy-start | bytes 786436
  9.5 22.3 %copy-start = (bf16[1,128,1024]{1,2,0:T(8,128)(2,1)}, bf16[1,128,1024]{1,2,0:T(8,128)(2,1)S(1)}, u32[]{:S(2)}) copy-start(bf16[1,128,1024]{1,2,0:T(8,128)(2,1)S(1)} %copy.64) | copy-start | bytes 786436
  10.3 21.5 %all-to-all-start.6 = ((bf16[128,32,32]{0,2,1:T(8,128)(2,1)}), bf16[128,32,32]{0,2,1:T(8,128)(2,1)S(1)}, u32[]{:S(2)}, u32[]{:S(2)}) async-start(bf16[128,32,32]{0,2,1:T(8,128)(2,1)} %bitcast.26), calls=%async_computation.6 | async-start | bytes 524288 | tf_op jit(solution)/shard_map/all_to_all | solution.py:96
  31.8 20.5 %all-to-all-start = ((bf16[256,32,32]{0,2,1:T(8,128)(2,1)}), bf16[256,32,32]{0,2,1:T(8,128)(2,1)S(1)}, u32[]{:S(2)}, u32[]{:S(2)}) async-start(bf16[256,32,32]{0,2,1:T(8,128)(2,1)} %pad_maximum_fusion.6), calls=%async_computation | async-start | bytes 1048576 | tf_op jit(solution)/shard_map/all_to_all | solution.py:96
  52.3 20.6 %all-to-all-start.7 = ((bf16[128,32,64]{0,2,1:T(8,128)(2,1)}), bf16[128,32,64]{0,2,1:T(8,128)(2,1)S(1)}, u32[]{:S(2)}, u32[]{:S(2)}) async-start(bf16[128,32,64]{0,2,1:T(8,128)(2,1)} %copy.68), calls=%async_computation.7 | async-start | bytes 1048576 | tf_op jit(solution)/shard_map/all_to_all | solution.py:100
  72.9 20.6 %all-to-all-start.8 = ((bf16[128,32,64]{0,2,1:T(8,128)(2,1)}), bf16[128,32,64]{0,2,1:T(8,128)(2,1)S(1)}, u32[]{:S(2)}, u32[]{:S(2)}) async-start(bf16[128,32,64]{0,2,1:T(8,128)(2,1)} %copy.71), calls=%async_computation.8 | async-start | bytes 1048576 | tf_op jit(solution)/shard_map/all_to_all | solution.py:101
  93.5 31.7 %all-to-all-start.2 = ((bf16[256,32,64]{0,2,1:T(8,128)(2,1)}), bf16[256,32,64]{0,2,1:T(8,128)(2,1)S(1)}, u32[]{:S(2)}, u32[]{:S(2)}) async-start(bf16[256,32,64]{0,2,1:T(8,128)(2,1)} %copy.55), calls=%async_computation.2 | async-start | bytes 2097152 | tf_op jit(solution)/shard_map/all_to_all | solution.py:101
  101.9 27.5 %copy-start.4 = (bf16[128,1024,2]{1,0,2:T(8,128)(2,1)S(1)}, bf16[128,1024,2]{1,0,2:T(8,128)(2,1)}, u32[]{:S(2)}) copy-start(bf16[128,1024,2]{1,0,2:T(8,128)(2,1)} %copy.69) | copy-start | bytes 1572868
  125.3 74.8 %all-to-all-start.1 = ((bf16[256,32,64]{0,2,1:T(8,128)(2,1)}), bf16[256,32,64]{0,2,1:T(8,128)(2,1)S(1)}, u32[]{:S(2)}, u32[]{:S(2)}) async-start(bf16[256,32,64]{0,2,1:T(8,128)(2,1)} %copy.52), calls=%async_computation.1 | async-start | bytes 2097152 | tf_op jit(solution)/shard_map/all_to_all | solution.py:100
  129.2 289.1 %all-reduce.3.cloned.1.call-start = ((), (), s32[]{:S(2)}) async-start(), calls=%async_computation.12 | async-start | bytes 2097152 | tf_op jit(solution)/shard_map/psum | solution.py:161
  146.8 17.0 %copy-start.14 = (f32[128,2,1024]{2,0,1:T(8,128)S(1)}, f32[128,2,1024]{2,0,1:T(8,128)}, u32[]{:S(2)}) copy-start(f32[128,2,1024]{2,0,1:T(8,128)} %fusion.12) | copy-start | bytes 3145732
  182.8 17.3 %copy-start.2 = (bf16[256,1024,2]{1,0,2:T(8,128)(2,1)}, bf16[256,1024,2]{1,0,2:T(8,128)(2,1)S(1)}, u32[]{:S(2)}) copy-start(bf16[256,1024,2]{1,0,2:T(8,128)(2,1)S(1)} %copy.56) | copy-start | bytes 3145732
  202.0 17.1 %copy-start.11 = (f32[256,2,1024]{2,0,1:T(8,128)S(1)}, f32[256,2,1024]{2,0,1:T(8,128)}, u32[]{:S(2)}) copy-start(f32[256,2,1024]{2,0,1:T(8,128)} %fusion.22) | copy-start | bytes 6291460
  219.1 16.7 %copy-start.3 = (bf16[256,1024,2]{1,0,2:T(8,128)(2,1)S(1)}, bf16[256,1024,2]{1,0,2:T(8,128)(2,1)}, u32[]{:S(2)}) copy-start(bf16[256,1024,2]{1,0,2:T(8,128)(2,1)} %copy-done.2) | copy-start | bytes 3145732
  235.8 16.7 %copy-start.5 = (bf16[128,1024,2]{1,0,2:T(8,128)(2,1)S(1)}, bf16[128,1024,2]{1,0,2:T(8,128)(2,1)}, u32[]{:S(2)}) copy-start(bf16[128,1024,2]{1,0,2:T(8,128)(2,1)} %copy.69) | copy-start | bytes 1572868
  235.8 16.7 %copy-start.13 = (f32[128,2,1024]{2,0,1:T(8,128)S(1)}, f32[128,2,1024]{2,0,1:T(8,128)}, u32[]{:S(2)}) copy-start(f32[128,2,1024]{2,0,1:T(8,128)} %fusion.61) | copy-start | bytes 3145732
  235.8 16.7 %copy-start.15 = (f32[128,2,1024]{2,0,1:T(8,128)S(1)}, f32[128,2,1024]{2,0,1:T(8,128)}, u32[]{:S(2)}) copy-start(f32[128,2,1024]{2,0,1:T(8,128)} %fusion.14) | copy-start | bytes 3145732
  336.7 81.5 %copy-start.16 = (bf16[128,2,1024]{2,0,1:T(8,128)(2,1)S(1)}, bf16[128,2,1024]{2,0,1:T(8,128)(2,1)}, u32[]{:S(2)}) copy-start(bf16[128,2,1024]{2,0,1:T(8,128)(2,1)} %get-tuple-element.14) | copy-start | bytes 1572868
  338.1 114.5 %all-to-all-start.4 = ((bf16[128,32,64]{0,2,1:T(8,128)(2,1)}), bf16[128,32,64]{0,2,1:T(8,128)(2,1)S(1)}, u32[]{:S(2)}, u32[]{:S(2)}) async-start(bf16[128,32,64]{0,2,1:T(8,128)(2,1)} %bitcast.17), calls=%async_computation.4 | async-start | bytes 1048576 | tf_op jit(solution)/shard_map/all_to_all | solution.py:128
  418.3 17.1 %copy-start.10 = (bf16[128,2,1024]{2,0,1:T(8,128)(2,1)S(1)}, bf16[128,2,1024]{2,0,1:T(8,128)(2,1)}, u32[]{:S(2)}) copy-start(bf16[128,2,1024]{2,0,1:T(8,128)(2,1)} %get-tuple-element.12) | copy-start | bytes 1572868
  418.3 17.1 %copy-start.17 = (bf16[128,2,1024]{2,0,1:T(8,128)(2,1)S(1)}, bf16[128,2,1024]{2,0,1:T(8,128)(2,1)}, u32[]{:S(2)}) copy-start(bf16[128,2,1024]{2,0,1:T(8,128)(2,1)} %get-tuple-element.17) | copy-start | bytes 1572868
  452.6 47.1 %all-to-all-start.3 = ((bf16[128,32,64]{0,2,1:T(8,128)(2,1)}), bf16[128,32,64]{0,2,1:T(8,128)(2,1)S(1)}, u32[]{:S(2)}, u32[]{:S(2)}) async-start(bf16[128,32,64]{0,2,1:T(8,128)(2,1)} %bitcast.11), calls=%async_computation.3 | async-start | bytes 1048576 | tf_op jit(solution)/shard_map/all_to_all | solution.py:127
  464.3 16.0 %copy-start.9 = (bf16[128,2,1024]{2,0,1:T(8,128)(2,1)S(1)}, bf16[128,2,1024]{2,0,1:T(8,128)(2,1)}, u32[]{:S(2)}) copy-start(bf16[128,2,1024]{2,0,1:T(8,128)(2,1)} %get-tuple-element.13) | copy-start | bytes 1572868
  464.3 16.0 %copy-start.12 = (f32[1024,256,2]{1,0,2:T(8,128)S(1)}, f32[1024,256,2]{1,0,2:T(8,128)}, u32[]{:S(2)}) copy-start(f32[1024,256,2]{1,0,2:T(8,128)} %fusion.46) | copy-start | bytes 6291460
  499.7 35.8 %all-to-all-start.10 = ((bf16[256,32,64]{0,2,1:T(8,128)(2,1)}), bf16[256,32,64]{0,2,1:T(8,128)(2,1)S(1)}, u32[]{:S(2)}, u32[]{:S(2)}) async-start(bf16[256,32,64]{0,2,1:T(8,128)(2,1)} %reshape.287), calls=%async_computation.10 | async-start | bytes 2097152 | tf_op jit(solution)/shard_map/all_to_all | solution.py:128
  535.5 31.9 %all-to-all-start.9 = ((bf16[256,32,64]{0,2,1:T(8,128)(2,1)}), bf16[256,32,64]{0,2,1:T(8,128)(2,1)S(1)}, u32[]{:S(2)}, u32[]{:S(2)}) async-start(bf16[256,32,64]{0,2,1:T(8,128)(2,1)} %reshape.285), calls=%async_computation.9 | async-start | bytes 2097152 | tf_op jit(solution)/shard_map/all_to_all | solution.py:127
  567.4 15.2 %all-to-all-start.5 = ((bf16[128,32,32]{0,2,1:T(8,128)(2,1)}), bf16[128,32,32]{0,2,1:T(8,128)(2,1)S(1)}, u32[]{:S(2)}, u32[]{:S(2)}) async-start(bf16[128,32,32]{0,2,1:T(8,128)(2,1)} %copy.63), calls=%async_computation.5 | async-start | bytes 524288 | tf_op jit(solution)/shard_map/all_to_all | solution.py:137
  571.8 1.1 copy-start.8
  573.0 13.3 %copy-start.1 = (bf16[1,128,1024]{1,2,0:T(8,128)(2,1)S(1)}, bf16[1,128,1024]{1,2,0:T(8,128)(2,1)}, u32[]{:S(2)}) copy-start(bf16[1,128,1024]{1,2,0:T(8,128)(2,1)} %copy-done) | copy-start | bytes 786436
  582.6 20.5 %all-to-all-start.11 = ((bf16[256,32,32]{0,2,1:T(8,128)(2,1)}), bf16[256,32,32]{0,2,1:T(8,128)(2,1)S(1)}, u32[]{:S(2)}, u32[]{:S(2)}) async-start(bf16[256,32,32]{0,2,1:T(8,128)(2,1)} %copy.79), calls=%async_computation.11 | async-start | bytes 1048576 | tf_op jit(solution)/shard_map/all_to_all | solution.py:137
Sparse Core Ops, SparseCore 0:
  287.2 130.9 all-reduce.2
where the time goes:
time: 620 us; the launch traced here: 612 us
  matrix products  278 us (45%)
  waiting for transfers between devices  218 us (35%)
  starting transfers between devices  68 us (11%)
  local copies, waits for them, and re-layouts  31.4 us (5%)
  between operations  15.1 us (2%)
    dot_general x8, matrix products, apply_table(): jnp.einsum('mqk,ql->mkl', member, matrix, preferred_element_type=jnp.floa...  137 us
    dot_general x8, matrix products, apply_table(): jnp.einsum('mkl,ql->mqk', member, matrix, preferred_element_type=jnp.floa...  133 us
    psum x1, waiting for transfers between devices, per_device(): lax.psum((spec_x[0] * spec_g[0] + spec_x[1] * spec_g[1]).astype(jnp.bfloa...  71 us
    all_to_all x2, waiting for transfers between devices, forward(): lax.all_to_all(halves[1], 'ctx', split_axis=1, concat_axis=1, tiled=True)  34.3 us
    all_to_all x2, waiting for transfers between devices, inverse(): lax.all_to_all(real_c, 'ctx', split_axis=1, concat_axis=1, tiled=True)  25.6 us
    all_to_all x2, waiting for transfers between devices, inverse(): lax.all_to_all(imag_c, 'ctx', split_axis=1, concat_axis=1, tiled=True)  24.2 us
    all_to_all x2, waiting for transfers between devices, forward(): lax.all_to_all(outgoing, 'ctx', split_axis=1, concat_axis=1, tiled=True)  23.9 us
    all_to_all x2, waiting for transfers between devices, inverse(): lax.all_to_all(outgoing, 'ctx', split_axis=1, concat_axis=1, tiled=True)  23 us
  transfers between devices with their start and end apart: 13, of which 10 were waited for; matrix products, arithmetic and copies ran while one was open for 36% of the time, Pallas kernels for 0%

commit v1 on v0

v1 whole, which is shorter than its diff:
```python
import functools
import math

import jax
import jax.numpy as jnp
import numpy as np
from jax import lax
from jax.experimental import pallas as pl
from jax.experimental.pallas import tpu as pltpu
from jax.sharding import PartitionSpec as P

MESH = pl.DeviceIdType.MESH
F32 = jnp.float32
BF16 = jnp.bfloat16

LANES = 128
ROWS = 256
LENGTH = ROWS * LANES
OWN = 4
UNITS = 8
SCALE = float(LENGTH) ** -1.5


def tables():
    place = np.arange(ROWS, dtype=np.float64)
    lane = np.arange(LANES, dtype=np.float64)
    outer = 2.0 * math.pi / ROWS * (place[:, None] + 0.25) * place[None, :]
    first = np.concatenate([np.cos(outer), -np.sin(outer)], axis=0)
    turn = 2.0 * math.pi / LENGTH * (place[:, None] + 0.25) * lane[None, :]
    inner = 2.0 * math.pi / LANES * lane[:, None] * lane[None, :]
    cos, sin = np.cos(inner), np.sin(inner)
    second = np.concatenate(
        [np.concatenate([cos, -sin], axis=1), np.concatenate([sin, cos], axis=1)], axis=0
    )
    as_b = lambda member: jnp.asarray(member.astype(np.float32)).astype(BF16)
    return (
        as_b(first),
        as_b(first.T),
        as_b(second),
        as_b(second.T),
        jnp.asarray(np.cos(turn).astype(np.float32)),
        jnp.asarray(np.sin(turn).astype(np.float32)),
    )


def kernel(
    ctx_size,
    dp_size,
    signal,
    gate,
    filt,
    cot,
    first,
    first_t,
    second,
    second_t,
    turn_cos,
    turn_sin,
    gated,
    grad_signal,
    grad_gate,
    grad_filter,
    out_buf,
    in_buf,
    stage,
    wide,
    lined,
    mixed,
    spec_h,
    spec_x,
    spec_g,
    send_sem,
    recv_sem,
    ready_sem,
):
    me = lax.axis_index("ctx")
    row = lax.axis_index("dp")
    per_row = ctx_size // dp_size
    SIG, FIL, MID, CNV, GRS, GRF = range(6)

    barrier = pltpu.get_barrier_semaphore()

    def greet_ctx(step, carry):
        peer = lax.rem(me + step, ctx_size)
        pl.semaphore_signal(barrier, inc=1, device_id=(row, peer), device_id_type=MESH)
        return carry

    def greet_dp(step, carry):
        peer = lax.rem(row + step, dp_size)
        pl.semaphore_signal(barrier, inc=1, device_id=(peer, me), device_id_type=MESH)
        return carry

    lax.fori_loop(1, ctx_size, greet_ctx, 0)
    lax.fori_loop(1, dp_size, greet_dp, 0)

    def split_channels(which, block):
        for unit in range(UNITS):
            stage[pl.ds(unit, ctx_size * OWN, stride=UNITS), :] = block(
                pl.ds(unit * LANES, LANES)
            )
        out_buf[which] = stage[...].reshape(ctx_size, OWN * UNITS, LANES).astype(BF16)

    def exchange(which):
        def send(step, carry):
            peer = lax.rem(me + step, ctx_size)
            pltpu.make_async_remote_copy(
                src_ref=out_buf.at[which, peer],
                dst_ref=in_buf.at[which, me],
                send_sem=send_sem.at[which],
                recv_sem=recv_sem.at[which],
                device_id=(row, peer),
                device_id_type=MESH,
            ).start()
            return carry

        lax.fori_loop(1, ctx_size, send, 0)
        in_buf[which, me] = out_buf[which, me]

    def wait_for(sem, which, count):
        part = in_buf.at[which, pl.ds(0, count)]
        pltpu.make_async_copy(part, part, sem.at[which]).wait()

    def transform(which, spec):
        for own in range(OWN):
            part = in_buf[which].astype(F32)[:, own * UNITS : (own + 1) * UNITS, :]
            lined[0:ROWS, own * LANES : (own + 1) * LANES] = part.reshape(ROWS, LANES).astype(BF16)
        wide[...] = jnp.dot(first[...], lined[0:ROWS, :], preferred_element_type=F32)
        for own in range(OWN):
            lanes = slice(own * LANES, (own + 1) * LANES)
            rows = slice(own * ROWS, (own + 1) * ROWS)
            real, imag = wide[0:ROWS, lanes], wide[ROWS : 2 * ROWS, lanes]
            cos, sin = turn_cos[...], turn_sin[...]
            mixed[rows, 0:LANES] = (real * cos + imag * sin).astype(BF16)
            mixed[rows, LANES : 2 * LANES] = (imag * cos - real * sin).astype(BF16)
        spec[...] = jnp.dot(mixed[...], second[...], preferred_element_type=F32)

    def multiply(left, right, conjugate):
        for own in range(OWN):
            rows = slice(own * ROWS, (own + 1) * ROWS)
            left_re, left_im = left[rows, 0:LANES], left[rows, LANES : 2 * LANES]
            right_re, right_im = right[rows, 0:LANES], right[rows, LANES : 2 * LANES]
            if conjugate:
                real = left_re * right_re + left_im * right_im
                imag = left_re * right_im - left_im * right_re
            else:
                real = left_re * right_re - left_im * right_im
                imag = left_re * right_im + left_im * right_re
            mixed[rows, 0:LANES] = real.astype(BF16)
            mixed[rows, LANES : 2 * LANES] = imag.astype(BF16)

    def transform_back(which):
        for own in range(OWN):
            lanes = slice(own * LANES, (own + 1) * LANES)
            rows = slice(own * ROWS, (own + 1) * ROWS)
            both = jnp.dot(mixed[rows, :], second_t[...], preferred_element_type=F32)
            real, imag = both[:, 0:LANES], both[:, LANES : 2 * LANES]
            cos, sin = turn_cos[...], turn_sin[...]
            lined[0:ROWS, lanes] = (real * cos - imag * sin).astype(BF16)
            lined[ROWS : 2 * ROWS, lanes] = (real * sin + imag * cos).astype(BF16)
        values = jnp.dot(first_t[...], lined[...], preferred_element_type=F32) * SCALE
        parts = [
            values[:, own * LANES : (own + 1) * LANES].reshape(ctx_size, UNITS, LANES)
            for own in range(OWN)
        ]
        out_buf[which] = jnp.concatenate(parts, axis=1).astype(BF16)

    def as_f32(ref):
        return lambda lanes: ref[:, lanes].astype(F32)

    split_channels(SIG, as_f32(signal))
    pl.semaphore_wait(barrier, ctx_size - 1 + dp_size - 1)

    def tell_ready(step, carry):
        peer = lax.rem(row + step, dp_size)
        pl.semaphore_signal(ready_sem, inc=1, device_id=(peer, me), device_id_type=MESH)
        return carry

    lax.fori_loop(1, dp_size, tell_ready, 0)

    exchange(SIG)
    split_channels(FIL, as_f32(filt))
    exchange(FIL)
    split_channels(MID, lambda lanes: gate[:, lanes].astype(F32) * cot[:, lanes].astype(F32))
    exchange(MID)

    wait_for(recv_sem, SIG, ctx_size - 1)
    transform(SIG, spec_x)
    wait_for(recv_sem, FIL, ctx_size - 1)
    transform(FIL, spec_h)
    multiply(spec_h, spec_x, False)
    transform_back(CNV)
    exchange(CNV)

    wait_for(recv_sem, MID, ctx_size - 1)
    transform(MID, spec_g)
    multiply(spec_x, spec_g, True)
    transform_back(GRF)
    pl.semaphore_wait(ready_sem, dp_size - 1)
    to_row = me // per_row
    slot = row * per_row + lax.rem(me, per_row)

    def send_filter(step, carry):
        peer = lax.rem(me + step, ctx_size)
        stays = jnp.logical_and(to_row == row, peer == me)

        @pl.when(jnp.logical_not(stays))
        def _():
            pltpu.make_async_remote_copy(
                src_ref=out_buf.at[GRF, peer],
                dst_ref=in_buf.at[GRF, slot],
                send_sem=send_sem.at[GRF],
                recv_sem=recv_sem.at[GRF],
                device_id=(to_row, peer),
                device_id_type=MESH,
            ).start()

        return carry

    lax.fori_loop(0, ctx_size, send_filter, 0)

    @pl.when(to_row == row)
    def _():
        in_buf[GRF, slot] = out_buf[GRF, me]

    multiply(spec_h, spec_g, True)
    transform_back(GRS)
    exchange(GRS)

    wait_for(recv_sem, CNV, ctx_size - 1)
    stage[...] = in_buf[CNV].astype(F32).reshape(ctx_size * OWN * UNITS, LANES)
    for unit in range(UNITS):
        lanes = pl.ds(unit * LANES, LANES)
        conv = stage[pl.ds(unit, ctx_size * OWN, stride=UNITS), :]
        gated[:, lanes] = (gate[:, lanes].astype(F32) * conv).astype(BF16)
        grad_gate[:, lanes] = (cot[:, lanes].astype(F32) * conv).astype(BF16)

    @pl.when(to_row == row)
    def _():
        wait_for(recv_sem, GRF, ctx_size - 1)

    @pl.when(to_row != row)
    def _():
        wait_for(recv_sem, GRF, ctx_size)

    share = per_row * OWN * UNITS
    total = in_buf[GRF, 0:per_row].astype(F32).reshape(share, LANES)
    for other in range(1, dp_size):
        part = in_buf[GRF, other * per_row : (other + 1) * per_row]
        total = total + part.astype(F32).reshape(share, LANES)
    stage[0:share, :] = total
    for unit in range(UNITS):
        lanes = pl.ds(unit * LANES, LANES)
        grad_filter[:, lanes] = stage[pl.ds(unit, per_row * OWN, stride=UNITS), :].astype(BF16)

    wait_for(recv_sem, GRS, ctx_size - 1)
    stage[...] = in_buf[GRS].astype(F32).reshape(ctx_size * OWN * UNITS, LANES)
    for unit in range(UNITS):
        lanes = pl.ds(unit * LANES, LANES)
        grad_signal[:, lanes] = stage[pl.ds(unit, ctx_size * OWN, stride=UNITS), :].astype(BF16)

    for which in (SIG, FIL, MID, CNV, GRS):
        wait_for(send_sem, which, ctx_size - 1)

    @pl.when(to_row == row)
    def _():
        wait_for(send_sem, GRF, ctx_size - 1)

    @pl.when(to_row != row)
    def _():
        wait_for(send_sem, GRF, ctx_size)


def per_device(signal, gate, filter_param, cotangent):
    ctx_size = lax.axis_size("ctx")
    dp_size = lax.axis_size("dp")
    channels, length = filter_param.shape
    block = jax.ShapeDtypeStruct((channels, length), BF16)
    share = jax.ShapeDtypeStruct((channels // dp_size, length), BF16)
    whole = pl.BlockSpec(memory_space=pltpu.VMEM)
    messages = (6, ctx_size, OWN * UNITS, LANES)
    outs = pl.pallas_call(
        functools.partial(kernel, ctx_size, dp_size),
        out_shape=(block, block, block, share),
        in_specs=[whole] * 10,
        out_specs=(whole,) * 4,
        scratch_shapes=[
            pltpu.VMEM(messages, BF16),
            pltpu.VMEM(messages, BF16),
            pltpu.VMEM((ctx_size * OWN * UNITS, LANES), F32),
            pltpu.VMEM((2 * ROWS, OWN * LANES), F32),
            pltpu.VMEM((2 * ROWS, OWN * LANES), BF16),
            pltpu.VMEM((OWN * ROWS, 2 * LANES), BF16),
            pltpu.VMEM((OWN * ROWS, 2 * LANES), F32),
            pltpu.VMEM((OWN * ROWS, 2 * LANES), F32),
            pltpu.VMEM((OWN * ROWS, 2 * LANES), F32),
            pltpu.SemaphoreType.DMA((6,)),
            pltpu.SemaphoreType.DMA((6,)),
            pltpu.SemaphoreType.REGULAR,
        ],
        compiler_params=pltpu.CompilerParams(
            collective_id=0, has_side_effects=True, vmem_limit_bytes=48 * 1024 * 1024
        ),
    )(
        signal.reshape(channels, length),
        gate.reshape(channels, length),
        filter_param,
        cotangent.reshape(channels, length),
        *tables(),
    )
    return (outs[0][None], outs[1][None], outs[2][None], outs[3])


def solution(mesh):
    in_specs = (P("dp", None, "ctx"), P("dp", None, "ctx"), P(None, "ctx"), P("dp", None, "ctx"))
    out_specs = (P("dp", None, "ctx"), P("dp", None, "ctx"), P("dp", None, "ctx"), P("dp", "ctx"))
    return jax.shard_map(
        per_device, mesh=mesh, in_specs=in_specs, out_specs=out_specs, check_vma=False
    )
```

time: 620 us -> 62.3 us (0.10); the launches traced: 612 us -> 61.9 us
  matrix products: 278 us -> 0 us
  waiting for transfers between devices: 218 us -> 0 us
  starting transfers between devices: 68 us -> 0 us
  Pallas kernels: 0 us -> 49.2 us
  local copies, waits for them, and re-layouts: 31.4 us -> 12 us
  between operations: 15.1 us -> 0.66 us
    dot_general x24 -> x0, matrix products: 278 us -> none  [the longest x8 137 us: apply_table(): jnp.einsum('mqk,ql->mkl', member, matrix, preferred_element_type=jnp.floa...]
    all_to_all x12 -> x0, waiting for transfers between devices: 147 us -> none  [the longest x2 34.3 us: forward(): lax.all_to_all(halves[1], 'ctx', split_axis=1, concat_axis=1, tiled=True)]
    psum x1 -> x0, waiting for transfers between devices: 71 us -> none  [per_device(): lax.psum((spec_x[0] * spec_g[0] + spec_x[1] * spec_g[1]).astype(jnp.bfloa...]
    all_to_all x12 -> x0, starting transfers between devices: 67.8 us -> none  [the longest x2 15.8 us: inverse(): lax.all_to_all(imag_c, 'ctx', split_axis=1, concat_axis=1, tiled=True)]
    pallas_call x0 -> x1, Pallas kernels: none -> 49.2 us  [per_device(): pl.pallas_call(functools.partial(kernel, ctx_size, dp_size), out_shape=(b...]
    reshape x20 -> x0, local copies, waits for them, and re-layouts: 17.3 us -> none  [the longest x4 5.16 us: regroup(): return member.reshape(number, cols_dev, ctx_size, freq_dev).transpose(0,...]
  transfers between devices with their start and end apart: 13 -> 0, of which waited for: 10 -> 0; matrix products, arithmetic and copies ran while one was open for 36% -> 0% of each run, Pallas kernels for 0% -> 0%
where the time goes in v1:
time: 62.3 us; the launch traced here: 61.9 us
  Pallas kernels  49.2 us (79%)
  local copies, waits for them, and re-layouts  12 us (19%)
  between operations  0.66 us (1%)
    pallas_call x1, Pallas kernels, per_device(): pl.pallas_call(functools.partial(kernel, ctx_size, dp_size), out_shape=(b...  49.2 us
    unnamed x24, local copies, waits for them, and re-layouts  12 us

profile of v1, /device:TPU:1, one launch (start us, length us, event | category | flops | bytes accessed | tf_op | source)
XLA Modules:
  0.0 61.9 jit_solution(1915000099459673808)
XLA Ops:
  0.6 0.0 copy-start
  0.6 0.9 %copy-done = bf16[1,128,1024]{2,1,0:T(8,128)(2,1)S(1)} copy-done((bf16[1,128,1024]{2,1,0:T(8,128)(2,1)S(1)}, bf16[1,128,1024]{2,1,0:T(8,128)(2,1)}, u32[]{:S(2)}) %copy-start) | copy-done | bytes 262168
  1.6 0.0 copy-start.1
  1.6 0.9 %copy-done.1 = bf16[1,128,1024]{2,1,0:T(8,128)(2,1)S(1)} copy-done((bf16[1,128,1024]{2,1,0:T(8,128)(2,1)S(1)}, bf16[1,128,1024]{2,1,0:T(8,128)(2,1)}, u32[]{:S(2)}) %copy-start.1) | copy-done | bytes 262168
  2.5 0.0 copy-start.2
  2.5 0.9 %copy-done.2 = bf16[128,1024]{1,0:T(8,128)(2,1)S(1)} copy-done((bf16[128,1024]{1,0:T(8,128)(2,1)S(1)}, bf16[128,1024]{1,0:T(8,128)(2,1)}, u32[]{:S(2)}) %copy-start.2) | copy-done | bytes 262168
  3.5 0.0 copy-start.3
  3.5 0.9 %copy-done.3 = bf16[1,128,1024]{2,1,0:T(8,128)(2,1)S(1)} copy-done((bf16[1,128,1024]{2,1,0:T(8,128)(2,1)S(1)}, bf16[1,128,1024]{2,1,0:T(8,128)(2,1)}, u32[]{:S(2)}) %copy-start.3) | copy-done | bytes 262168
  4.4 0.0 copy-start.4
  4.4 0.9 %copy-done.4 = bf16[256,512]{1,0:T(8,128)(2,1)S(1)} copy-done((bf16[256,512]{1,0:T(8,128)(2,1)S(1)}, bf16[256,512]{1,0:T(8,128)(2,1)}, u32[]{:S(2)}) %copy-start.4) | copy-done | bytes 262168
  5.4 0.0 copy-start.5
  5.4 0.9 %copy-done.5 = bf16[512,256]{1,0:T(8,128)(2,1)S(1)} copy-done((bf16[512,256]{1,0:T(8,128)(2,1)S(1)}, bf16[512,256]{1,0:T(8,128)(2,1)}, u32[]{:S(2)}) %copy-start.5) | copy-done | bytes 262168
  6.3 0.0 copy-start.6
  6.3 0.9 %copy-done.6 = bf16[256,256]{1,0:T(8,128)(2,1)S(1)} copy-done((bf16[256,256]{1,0:T(8,128)(2,1)S(1)}, bf16[256,256]{1,0:T(8,128)(2,1)}, u32[]{:S(2)}) %copy-start.6) | copy-done | bytes 131096
  7.2 0.0 copy-start.7
  7.2 0.9 %copy-done.7 = bf16[256,256]{1,0:T(8,128)(2,1)S(1)} copy-done((bf16[256,256]{1,0:T(8,128)(2,1)S(1)}, bf16[256,256]{1,0:T(8,128)(2,1)}, u32[]{:S(2)}) %copy-start.7) | copy-done | bytes 131096
  8.1 0.0 copy-start.8
  8.1 0.9 %copy-done.8 = f32[256,128]{1,0:T(8,128)S(1)} copy-done((f32[256,128]{1,0:T(8,128)S(1)}, f32[256,128]{1,0:T(8,128)}, u32[]{:S(2)}) %copy-start.8) | copy-done | bytes 131096
  9.0 0.0 copy-start.9
  9.1 0.9 %copy-done.9 = f32[256,128]{1,0:T(8,128)S(1)} copy-done((f32[256,128]{1,0:T(8,128)S(1)}, f32[256,128]{1,0:T(8,128)}, u32[]{:S(2)}) %copy-start.9) | copy-done | bytes 131096
  10.0 49.2 %shard_map.129 = (bf16[128,1024]{1,0:T(8,128)(2,1)S(1)}, bf16[128,1024]{1,0:T(8,128)(2,1)S(1)}, bf16[128,1024]{1,0:T(8,128)(2,1)S(1)}, bf16[16,1024]{1,0:T(8,128)(2,1)S(1)}) custom-call(bf16[128,1024]{1,0:T(8,128)(2,1)S(1)} %bitcast.9, bf16[128,1024]{1,0:T(8,128)(2,1)S(1)} %bitcast.10, bf16[128,1024]{1,0:T(8,128)(2,1)S(1)} %copy-done.2, ...), custom_call_target="tpu_custom_call" | custom-call | tf_op jit(solution)/shard_map/pallas_call | solution.py:281
  59.2 0.7 %copy.18 = bf16[1,128,1024]{2,1,0:T(8,128)(2,1)} copy(bf16[1,128,1024]{2,1,0:T(8,128)(2,1)S(1)} %bitcast.8) | data formatting | bytes 524288
  59.9 0.7 %copy.19 = bf16[1,128,1024]{2,1,0:T(8,128)(2,1)} copy(bf16[1,128,1024]{2,1,0:T(8,128)(2,1)S(1)} %bitcast.7) | data formatting | bytes 524288
  60.6 0.7 %copy.20 = bf16[1,128,1024]{2,1,0:T(8,128)(2,1)} copy(bf16[1,128,1024]{2,1,0:T(8,128)(2,1)S(1)} %bitcast.6) | data formatting | bytes 524288
  61.3 0.6 copy.21
Async XLA Ops:
  0.6 1.0 %copy-start = (bf16[1,128,1024]{2,1,0:T(8,128)(2,1)S(1)}, bf16[1,128,1024]{2,1,0:T(8,128)(2,1)}, u32[]{:S(2)}) copy-start(bf16[1,128,1024]{2,1,0:T(8,128)(2,1)} %param.10) | copy-start | bytes 786436
  1.6 0.9 %copy-start.1 = (bf16[1,128,1024]{2,1,0:T(8,128)(2,1)S(1)}, bf16[1,128,1024]{2,1,0:T(8,128)(2,1)}, u32[]{:S(2)}) copy-start(bf16[1,128,1024]{2,1,0:T(8,128)(2,1)} %param.11) | copy-start | bytes 786436
  2.5 0.9 %copy-start.2 = (bf16[128,1024]{1,0:T(8,128)(2,1)S(1)}, bf16[128,1024]{1,0:T(8,128)(2,1)}, u32[]{:S(2)}) copy-start(bf16[128,1024]{1,0:T(8,128)(2,1)} %filt.1) | copy-start | bytes 786436
  3.5 0.9 %copy-start.3 = (bf16[1,128,1024]{2,1,0:T(8,128)(2,1)S(1)}, bf16[1,128,1024]{2,1,0:T(8,128)(2,1)}, u32[]{:S(2)}) copy-start(bf16[1,128,1024]{2,1,0:T(8,128)(2,1)} %param.13) | copy-start | bytes 786436
  4.4 0.9 %copy-start.4 = (bf16[256,512]{1,0:T(8,128)(2,1)S(1)}, bf16[256,512]{1,0:T(8,128)(2,1)}, u32[]{:S(2)}) copy-start(bf16[256,512]{1,0:T(8,128)(2,1)} %constant.22.first_t) | copy-start | bytes 786436
  5.4 0.9 %copy-start.5 = (bf16[512,256]{1,0:T(8,128)(2,1)S(1)}, bf16[512,256]{1,0:T(8,128)(2,1)}, u32[]{:S(2)}) copy-start(bf16[512,256]{1,0:T(8,128)(2,1)} %constant.21.first) | copy-start | bytes 786436
  6.3 0.9 %copy-start.6 = (bf16[256,256]{1,0:T(8,128)(2,1)S(1)}, bf16[256,256]{1,0:T(8,128)(2,1)}, u32[]{:S(2)}) copy-start(bf16[256,256]{1,0:T(8,128)(2,1)} %constant.24.second_t) | copy-start | bytes 393220
  7.2 0.9 %copy-start.7 = (bf16[256,256]{1,0:T(8,128)(2,1)S(1)}, bf16[256,256]{1,0:T(8,128)(2,1)}, u32[]{:S(2)}) copy-start(bf16[256,256]{1,0:T(8,128)(2,1)} %constant.23.second) | copy-start | bytes 393220
  8.1 0.9 %copy-start.8 = (f32[256,128]{1,0:T(8,128)S(1)}, f32[256,128]{1,0:T(8,128)}, u32[]{:S(2)}) copy-start(f32[256,128]{1,0:T(8,128)} %constant.17.clone.turn_sin) | copy-start | bytes 393220
  9.0 0.9 %copy-start.9 = (f32[256,128]{1,0:T(8,128)S(1)}, f32[256,128]{1,0:T(8,128)}, u32[]{:S(2)}) copy-start(f32[256,128]{1,0:T(8,128)} %constant.16.clone.turn_cos) | copy-start | bytes 393220

commit v2 on v1

v2 whole, which is shorter than its diff:
```python
import functools
import math

import jax
import jax.numpy as jnp
import numpy as np
from jax import lax
from jax.experimental import pallas as pl
from jax.experimental.pallas import tpu as pltpu
from jax.sharding import PartitionSpec as P

MESH = pl.DeviceIdType.MESH
F32 = jnp.float32
BF16 = jnp.bfloat16

LANES = 128
ROWS = 256
LENGTH = ROWS * LANES
OWN = 4
UNITS = 8
SCALE = float(LENGTH) ** -1.5


def tables():
    place = np.arange(ROWS, dtype=np.float64)
    lane = np.arange(LANES, dtype=np.float64)
    outer = 2.0 * math.pi / ROWS * (place[:, None] + 0.25) * place[None, :]
    first = np.concatenate([np.cos(outer), -np.sin(outer)], axis=0)
    turn = 2.0 * math.pi / LENGTH * (place[:, None] + 0.25) * lane[None, :]
    inner = 2.0 * math.pi / LANES * lane[:, None] * lane[None, :]
    cos, sin = np.cos(inner), np.sin(inner)
    second = np.concatenate(
        [np.concatenate([cos, -sin], axis=1), np.concatenate([sin, cos], axis=1)], axis=0
    )
    as_b = lambda member: jnp.asarray(member.astype(np.float32)).astype(BF16)
    return (
        as_b(first),
        as_b(first.T),
        as_b(second),
        as_b(second.T),
        jnp.asarray(np.cos(turn).astype(np.float32)),
        jnp.asarray(np.sin(turn).astype(np.float32)),
    )


def kernel(
    ctx_size,
    dp_size,
    signal_hbm,
    gate_hbm,
    filt_hbm,
    cot_hbm,
    first_hbm,
    first_t_hbm,
    second_hbm,
    second_t_hbm,
    turn_cos_hbm,
    turn_sin_hbm,
    gated,
    grad_signal,
    grad_gate,
    grad_filter,
    signal,
    gate,
    filt,
    cot,
    first,
    first_t,
    second,
    second_t,
    turn_cos,
    turn_sin,
    out_buf,
    in_buf,
    in_filt,
    in_part,
    out_sum,
    in_sum,
    stage,
    wide,
    lined,
    mixed,
    spec_h,
    spec_x,
    spec_g,
    send_sem,
    recv_sem,
    load_sem,
):
    me = lax.axis_index("ctx")
    row = lax.axis_index("dp")
    per_row = ctx_size // dp_size
    lanes_x = dp_size // 2
    my_x, my_z = row // 2, lax.rem(row, 2)
    share = ctx_size // lanes_x
    my_y, my_low = me // share, lax.rem(me, share) // 2
    SIG, MID, CNV, GRS, FIL, GRF = range(6)
    FIL_X, GRF_X = 6, 7

    loads = [
        pltpu.make_async_copy(source, target, load_sem.at[index])
        for index, (source, target) in enumerate(
            (
                (filt_hbm, filt),
                (signal_hbm, signal),
                (gate_hbm, gate),
                (cot_hbm, cot),
                (first_hbm, first),
                (turn_cos_hbm, turn_cos),
                (turn_sin_hbm, turn_sin),
                (second_hbm, second),
                (second_t_hbm, second_t),
                (first_t_hbm, first_t),
            )
        )
    ]

    barrier = pltpu.get_barrier_semaphore()

    def greet_ctx(step, carry):
        peer = lax.rem(me + step, ctx_size)
        pl.semaphore_signal(barrier, inc=1, device_id=(row, peer), device_id_type=MESH)
        return carry

    lax.fori_loop(1, ctx_size, greet_ctx, 0)
    for step in range(1, lanes_x):
        peer = lax.rem(my_x + step, lanes_x) * 2 + my_z
        pl.semaphore_signal(barrier, inc=1, device_id=(peer, me), device_id_type=MESH)
    other = my_x * 2 + 1 - my_z
    pl.semaphore_signal(barrier, inc=1, device_id=(other, me), device_id_type=MESH)

    for copy in loads:
        copy.start()

    def split_channels(which, block):
        for unit in range(UNITS):
            stage[pl.ds(unit, ctx_size * OWN, stride=UNITS), :] = block(
                pl.ds(unit * LANES, LANES)
            )
        out_buf[which] = stage[...].reshape(ctx_size, OWN * UNITS, LANES).astype(BF16)

    def remote(source, target, sem, device):
        pltpu.make_async_remote_copy(
            src_ref=source,
            dst_ref=target,
            send_sem=send_sem.at[sem],
            recv_sem=recv_sem.at[sem],
            device_id=device,
            device_id_type=MESH,
        ).start()

    def exchange(which):
        def send(step, carry):
            peer = lax.rem(me + step, ctx_size)
            remote(out_buf.at[which, peer], in_buf.at[which, me], which, (row, peer))
            return carry

        lax.fori_loop(1, ctx_size, send, 0)
        in_buf[which, me] = out_buf[which, me]

    def wait_for(sem, which, count):
        part = in_buf.at[0, pl.ds(0, count)]
        pltpu.make_async_copy(part, part, sem.at[which]).wait()

    def wait_either(sem, which, count, less):
        @pl.when(less)
        def _():
            wait_for(sem, which, count - 1)

        @pl.when(jnp.logical_not(less))
        def _():
            wait_for(sem, which, count)

    def line_up(part, block, blocks):
        part = part.astype(F32)
        for own in range(OWN):
            rows = part[:, own * UNITS : (own + 1) * UNITS, :].reshape(blocks * UNITS, LANES)
            lined[
                block * UNITS : (block + blocks) * UNITS, own * LANES : (own + 1) * LANES
            ] = rows.astype(BF16)

    def transform(spec):
        wide[...] = jnp.dot(first[...], lined[0:ROWS, :], preferred_element_type=F32)
        for own in range(OWN):
            lanes = slice(own * LANES, (own + 1) * LANES)
            rows = slice(own * ROWS, (own + 1) * ROWS)
            real, imag = wide[0:ROWS, lanes], wide[ROWS : 2 * ROWS, lanes]
            cos, sin = turn_cos[...], turn_sin[...]
            mixed[rows, 0:LANES] = (real * cos + imag * sin).astype(BF16)
            mixed[rows, LANES : 2 * LANES] = (imag * cos - real * sin).astype(BF16)
        spec[...] = jnp.dot(mixed[...], second[...], preferred_element_type=F32)

    def multiply(left, right, conjugate):
        for own in range(OWN):
            rows = slice(own * ROWS, (own + 1) * ROWS)
            left_re, left_im = left[rows, 0:LANES], left[rows, LANES : 2 * LANES]
            right_re, right_im = right[rows, 0:LANES], right[rows, LANES : 2 * LANES]
            if conjugate:
                real = left_re * right_re + left_im * right_im
                imag = left_re * right_im - left_im * right_re
            else:
                real = left_re * right_re - left_im * right_im
                imag = left_re * right_im + left_im * right_re
            mixed[rows, 0:LANES] = real.astype(BF16)
            mixed[rows, LANES : 2 * LANES] = imag.astype(BF16)

    def transform_back(which):
        for own in range(OWN):
            lanes = slice(own * LANES, (own + 1) * LANES)
            rows = slice(own * ROWS, (own + 1) * ROWS)
            both = jnp.dot(mixed[rows, :], second_t[...], preferred_element_type=F32)
            real, imag = both[:, 0:LANES], both[:, LANES : 2 * LANES]
            cos, sin = turn_cos[...], turn_sin[...]
            lined[0:ROWS, lanes] = (real * cos - imag * sin).astype(BF16)
            lined[ROWS : 2 * ROWS, lanes] = (real * sin + imag * cos).astype(BF16)
        values = jnp.dot(first_t[...], lined[...], preferred_element_type=F32) * SCALE
        parts = [
            values[:, own * LANES : (own + 1) * LANES].reshape(ctx_size, UNITS, LANES)
            for own in range(OWN)
        ]
        out_buf[which] = jnp.concatenate(parts, axis=1).astype(BF16)

    fetches = lax.rem(my_y + my_low, lanes_x) == my_x
    filt_slot = 2 * my_y + lax.rem(me, 2)

    loads[0].wait()

    @pl.when(fetches)
    def _():
        split_channels(FIL, lambda lanes: filt[:, lanes].astype(F32))

    loads[1].wait()
    split_channels(SIG, lambda lanes: signal[:, lanes].astype(F32))
    pl.semaphore_wait(barrier, ctx_size - 1 + lanes_x)

    @pl.when(fetches)
    def _():
        def send(step, carry):
            peer = lax.rem(me + step, ctx_size)
            remote(out_buf.at[FIL, peer], in_filt.at[my_x, filt_slot], FIL, (row, peer))
            return carry

        lax.fori_loop(1, ctx_size, send, 0)
        in_filt[my_x, filt_slot] = out_buf[FIL, me]

    exchange(SIG)
    loads[2].wait()
    loads[3].wait()
    split_channels(MID, lambda lanes: gate[:, lanes].astype(F32) * cot[:, lanes].astype(F32))
    wait_either(recv_sem, FIL, share, fetches)
    for step in range(1, lanes_x):
        peer = lax.rem(my_x + step, lanes_x) * 2 + my_z
        remote(in_filt.at[my_x], in_filt.at[my_x], FIL_X, (peer, me))
    exchange(MID)

    for copy in loads[4:]:
        copy.wait()
    wait_for(recv_sem, SIG, ctx_size - 1)
    line_up(in_buf[SIG], 0, ctx_size)
    transform(spec_x)
    wait_for(recv_sem, FIL_X, share * (lanes_x - 1))
    for pair in range(ctx_size // 2):
        part_y, part_low = pair // (share // 2), pair % (share // 2)
        group = (part_y + part_low) % lanes_x
        line_up(in_filt[group, 2 * part_y : 2 * part_y + 2], 2 * pair, 2)
    transform(spec_h)
    multiply(spec_h, spec_x, False)
    transform_back(CNV)
    exchange(CNV)

    wait_for(recv_sem, MID, ctx_size - 1)
    line_up(in_buf[MID], 0, ctx_size)
    transform(spec_g)
    multiply(spec_x, spec_g, True)
    transform_back(GRF)
    for step in range(1, lanes_x):
        peer = lax.rem(my_x + step, lanes_x)
        blocks = out_buf.at[GRF, pl.ds(peer * share, share)]
        remote(blocks, in_part.at[my_x], GRF_X, (peer * 2 + my_z, me))
    in_part[my_x] = out_buf[GRF, pl.ds(my_x * share, share)]

    multiply(spec_h, spec_g, True)
    transform_back(GRS)
    exchange(GRS)

    wait_for(recv_sem, GRF_X, share * (lanes_x - 1))
    total = in_part[0].astype(F32)
    for part in range(1, lanes_x):
        total = total + in_part[part].astype(F32)
    out_sum[...] = total.astype(BF16)
    to_row = me // per_row
    slot = my_z * per_row + lax.rem(me, per_row)
    stays = jnp.logical_and(to_row == row, me // share == my_x)

    def send_sum(block, carry):
        peer = my_x * share + block
        leaves = jnp.logical_or(to_row != row, peer != me)

        @pl.when(leaves)
        def _():
            remote(out_sum.at[block], in_sum.at[slot], GRF, (to_row, peer))

        return carry

    lax.fori_loop(0, share, send_sum, 0)

    @pl.when(stays)
    def _():
        in_sum[slot] = out_sum[lax.rem(me, share)]

    wait_for(recv_sem, CNV, ctx_size - 1)
    stage[...] = in_buf[CNV].astype(F32).reshape(ctx_size * OWN * UNITS, LANES)
    for unit in range(UNITS):
        lanes = pl.ds(unit * LANES, LANES)
        conv = stage[pl.ds(unit, ctx_size * OWN, stride=UNITS), :]
        gated[:, lanes] = (gate[:, lanes].astype(F32) * conv).astype(BF16)
        grad_gate[:, lanes] = (cot[:, lanes].astype(F32) * conv).astype(BF16)

    wait_either(recv_sem, GRF, 2 * per_row, stays)
    total = in_sum[0:per_row].astype(F32) + in_sum[per_row : 2 * per_row].astype(F32)
    stage[0 : per_row * OWN * UNITS, :] = total.reshape(per_row * OWN * UNITS, LANES)
    for unit in range(UNITS):
        lanes = pl.ds(unit * LANES, LANES)
        grad_filter[:, lanes] = stage[pl.ds(unit, per_row * OWN, stride=UNITS), :].astype(BF16)

    wait_for(recv_sem, GRS, ctx_size - 1)
    stage[...] = in_buf[GRS].astype(F32).reshape(ctx_size * OWN * UNITS, LANES)
    for unit in range(UNITS):
        lanes = pl.ds(unit * LANES, LANES)
        grad_signal[:, lanes] = stage[pl.ds(unit, ctx_size * OWN, stride=UNITS), :].astype(BF16)

    for which in (SIG, MID, CNV, GRS):
        wait_for(send_sem, which, ctx_size - 1)
    for which in (FIL_X, GRF_X):
        wait_for(send_sem, which, share * (lanes_x - 1))
    wait_either(send_sem, GRF, share, stays)

    @pl.when(fetches)
    def _():
        wait_for(send_sem, FIL, ctx_size - 1)


def hand_on(*refs):
    sources, targets, sem = refs[0:4], refs[4:8], refs[8]
    copies = [
        pltpu.make_async_copy(source, target, sem.at[index])
        for index, (source, target) in enumerate(zip(sources, targets))
    ]
    for copy in copies:
        copy.start()
    for copy in copies:
        copy.wait()


def per_device(signal, gate, filter_param, cotangent):
    ctx_size = lax.axis_size("ctx")
    dp_size = lax.axis_size("dp")
    channels, length = filter_param.shape
    lanes_x = dp_size // 2
    share = ctx_size // lanes_x
    block = (channels, length)
    part = (channels // dp_size, length)
    outer = pl.BlockSpec(memory_space=pltpu.HBM)
    inner = pl.BlockSpec(memory_space=pltpu.VMEM)
    message = (OWN * UNITS, LANES)
    spectrum = pltpu.VMEM((OWN * ROWS, 2 * LANES), F32)
    outs = pl.pallas_call(
        functools.partial(kernel, ctx_size, dp_size),
        out_shape=tuple(pltpu.VMEM(shape, BF16) for shape in (block, block, block, part)),
        in_specs=[outer] * 10,
        out_specs=(inner,) * 4,
        scratch_shapes=[
            pltpu.VMEM(block, BF16),
            pltpu.VMEM(block, BF16),
            pltpu.VMEM(block, BF16),
            pltpu.VMEM(block, BF16),
            pltpu.VMEM((2 * ROWS, ROWS), BF16),
            pltpu.VMEM((ROWS, 2 * ROWS), BF16),
            pltpu.VMEM((2 * LANES, 2 * LANES), BF16),
            pltpu.VMEM((2 * LANES, 2 * LANES), BF16),
            pltpu.VMEM((ROWS, LANES), F32),
            pltpu.VMEM((ROWS, LANES), F32),
            pltpu.VMEM((6, ctx_size) + message, BF16),
            pltpu.VMEM((4, ctx_size) + message, BF16),
            pltpu.VMEM((lanes_x, share) + message, BF16),
            pltpu.VMEM((lanes_x, share) + message, BF16),
            pltpu.VMEM((share,) + message, BF16),
            pltpu.VMEM((2 * ctx_size // dp_size,) + message, BF16),
            pltpu.VMEM((ctx_size * OWN * UNITS, LANES), F32),
            pltpu.VMEM((2 * ROWS, OWN * LANES), F32),
            pltpu.VMEM((2 * ROWS, OWN * LANES), BF16),
            pltpu.VMEM((OWN * ROWS, 2 * LANES), BF16),
            spectrum,
            spectrum,
            spectrum,
            pltpu.SemaphoreType.DMA((8,)),
            pltpu.SemaphoreType.DMA((8,)),
            pltpu.SemaphoreType.DMA((10,)),
        ],
        compiler_params=pltpu.CompilerParams(
            collective_id=0, has_side_effects=True, vmem_limit_bytes=60 * 1024 * 1024
        ),
    )(
        signal.reshape(block),
        gate.reshape(block),
        filter_param,
        cotangent.reshape(block),
        *tables(),
    )
    outs = pl.pallas_call(
        hand_on,
        out_shape=tuple(jax.ShapeDtypeStruct(shape, BF16) for shape in (block, block, block, part)),
        in_specs=[inner] * 4,
        out_specs=(outer,) * 4,
        scratch_shapes=[pltpu.SemaphoreType.DMA((4,))],
    )(*outs)
    return (outs[0][None], outs[1][None], outs[2][None], outs[3])


def solution(mesh):
    in_specs = (P("dp", None, "ctx"), P("dp", None, "ctx"), P(None, "ctx"), P("dp", None, "ctx"))
    out_specs = (P("dp", None, "ctx"), P("dp", None, "ctx"), P("dp", None, "ctx"), P("dp", "ctx"))
    return jax.shard_map(
        per_device, mesh=mesh, in_specs=in_specs, out_specs=out_specs, check_vma=False
    )
```

time: 62.3 us -> 47.7 us (0.77)
  local copies, waits for them, and re-layouts: 12 us -> 2.68 us
  Pallas kernels: 49.2 us -> 43.7 us
    unnamed x24 -> x8, local copies, waits for them, and re-layouts: 12 us -> 2.68 us
    pallas_call x1 -> x2, Pallas kernels: 49.2 us -> 43.7 us  [the longest x1 41.7 us: per_device(): pl.pallas_call(functools.partial(kernel, ctx_size, dp_size), out_shape=tu...]
where the time goes in v2:
time: 47.7 us; the launch traced here: 47 us
  Pallas kernels  43.7 us (92%)
  local copies, waits for them, and re-layouts  2.68 us (6%)
  between operations  0.65 us (1%)
    pallas_call x1, Pallas kernels, per_device(): pl.pallas_call(functools.partial(kernel, ctx_size, dp_size), out_shape=tu...  41.7 us
    unnamed x8, local copies, waits for them, and re-layouts  2.68 us
    pallas_call x1, Pallas kernels, per_device(): pl.pallas_call(hand_on, out_shape=tuple((jax.ShapeDtypeStruct(shape, BF16...  2.02 us

profile of v2, /device:TPU:1, one launch (start us, length us, event | category | flops | bytes accessed | tf_op | source)
XLA Modules:
  0.0 47.0 jit_solution(3856966159953975202)
XLA Ops:
  0.6 41.7 %shard_map.129 = (bf16[128,1024]{1,0:T(8,128)(2,1)S(1)}, bf16[128,1024]{1,0:T(8,128)(2,1)S(1)}, bf16[128,1024]{1,0:T(8,128)(2,1)S(1)}, bf16[16,1024]{1,0:T(8,128)(2,1)S(1)}) custom-call(bf16[128,1024]{1,0:T(8,128)(2,1)} %bitcast.6, bf16[128,1024]{1,0:T(8,128)(2,1)} %bitcast.7, bf16[128,1024]{1,0:T(8,128)(2,1)} %filt_hbm.1, bf16[128,1024]{1,0:T(8,128)(2,1)} %bitcast.8, ...), custom_call_target="tpu_custom_call" | custom-call | tf_op jit(solution)/shard_map/pallas_call | solution.py:367
  42.3 0.0 copy-start
  42.3 0.7 %copy-done = bf16[128,1024]{1,0:T(8,128)(2,1)} copy-done((bf16[128,1024]{1,0:T(8,128)(2,1)}, bf16[128,1024]{1,0:T(8,128)(2,1)S(1)}, u32[]{:S(2)}) %copy-start) | copy-done | bytes 262168
  43.0 0.0 copy-start.1
  43.0 0.7 %copy-done.1 = bf16[128,1024]{1,0:T(8,128)(2,1)} copy-done((bf16[128,1024]{1,0:T(8,128)(2,1)}, bf16[128,1024]{1,0:T(8,128)(2,1)S(1)}, u32[]{:S(2)}) %copy-start.1) | copy-done | bytes 262168
  43.7 0.0 copy-start.2
  43.7 0.7 %copy-done.2 = bf16[128,1024]{1,0:T(8,128)(2,1)} copy-done((bf16[128,1024]{1,0:T(8,128)(2,1)}, bf16[128,1024]{1,0:T(8,128)(2,1)S(1)}, u32[]{:S(2)}) %copy-start.2) | copy-done | bytes 262168
  44.4 0.0 copy-start.3
  44.4 0.6 %copy-done.3 = bf16[16,1024]{1,0:T(8,128)(2,1)} copy-done((bf16[16,1024]{1,0:T(8,128)(2,1)}, bf16[16,1024]{1,0:T(8,128)(2,1)S(1)}, u32[]{:S(2)}) %copy-start.3) | copy-done | bytes 32792
  45.0 2.0 %shard_map.130 = (bf16[128,1024]{1,0:T(8,128)(2,1)}, bf16[128,1024]{1,0:T(8,128)(2,1)}, bf16[128,1024]{1,0:T(8,128)(2,1)}, bf16[16,1024]{1,0:T(8,128)(2,1)}) custom-call(bf16[128,1024]{1,0:T(8,128)(2,1)} %copy-done, bf16[128,1024]{1,0:T(8,128)(2,1)} %copy-done.1, bf16[128,1024]{1,0:T(8,128)(2,1)} %copy-done.2, bf16[16,1024]{1,0:T(8,128)(2,1)} %copy-done.3), custom_call_target="tpu_custom_call" | custom-call | tf_op jit(solution)/shard_map/pallas_call | solution.py:410
Async XLA Ops:
  42.3 0.7 %copy-start = (bf16[128,1024]{1,0:T(8,128)(2,1)}, bf16[128,1024]{1,0:T(8,128)(2,1)S(1)}, u32[]{:S(2)}) copy-start(bf16[128,1024]{1,0:T(8,128)(2,1)S(1)} %get-tuple-element.12.refs_0_) | copy-start | bytes 786436
  43.0 0.7 %copy-start.1 = (bf16[128,1024]{1,0:T(8,128)(2,1)}, bf16[128,1024]{1,0:T(8,128)(2,1)S(1)}, u32[]{:S(2)}) copy-start(bf16[128,1024]{1,0:T(8,128)(2,1)S(1)} %get-tuple-element.13.refs_1_) | copy-start | bytes 786436
  43.7 0.7 %copy-start.2 = (bf16[128,1024]{1,0:T(8,128)(2,1)}, bf16[128,1024]{1,0:T(8,128)(2,1)S(1)}, u32[]{:S(2)}) copy-start(bf16[128,1024]{1,0:T(8,128)(2,1)S(1)} %get-tuple-element.14.refs_2_) | copy-start | bytes 786436
  44.4 0.6 %copy-start.3 = (bf16[16,1024]{1,0:T(8,128)(2,1)}, bf16[16,1024]{1,0:T(8,128)(2,1)S(1)}, u32[]{:S(2)}) copy-start(bf16[16,1024]{1,0:T(8,128)(2,1)S(1)} %get-tuple-element.15.refs_3_) | copy-start | bytes 98308

commit v3 on v2

--- a/solution.py
+++ b/solution.py
@@ -413,6 +413,7 @@
         in_specs=[inner] * 4,
         out_specs=(outer,) * 4,
         scratch_shapes=[pltpu.SemaphoreType.DMA((4,))],
+        compiler_params=pltpu.CompilerParams(vmem_limit_bytes=4 * 1024 * 1024),
     )(*outs)
     return (outs[0][None], outs[1][None], outs[2][None], outs[3])
 

time: 47.7 us -> 43.9 us (0.920)
  local copies, waits for them, and re-layouts: 2.68 us -> 0 us
  Pallas kernels: 43.7 us -> 42.6 us
    unnamed x8 -> x0, local copies, waits for them, and re-layouts: 2.68 us -> none
    pallas_call x1, Pallas kernels: 2.02 us -> 0.91 us  [per_device(): pl.pallas_call(hand_on, out_shape=tuple((jax.ShapeDtypeStruct(shape, BF16...]
where the time goes in v3:
time: 43.9 us; the launch traced here: 43.2 us
  Pallas kernels  42.6 us (97%)
  between operations  0.64 us (1%)
    pallas_call x1, Pallas kernels, per_device(): pl.pallas_call(functools.partial(kernel, ctx_size, dp_size), out_shape=tu...  41.7 us
    pallas_call x1, Pallas kernels, per_device(): pl.pallas_call(hand_on, out_shape=tuple((jax.ShapeDtypeStruct(shape, BF16...  0.91 us

profile of v3, /device:TPU:1, one launch (start us, length us, event | category | flops | bytes accessed | tf_op | source)
XLA Modules:
  0.0 43.2 jit_solution(11130568606483638220)
XLA Ops:
  0.6 41.7 %shard_map.129 = (bf16[128,1024]{1,0:T(8,128)(2,1)S(1)}, bf16[128,1024]{1,0:T(8,128)(2,1)S(1)}, bf16[128,1024]{1,0:T(8,128)(2,1)S(1)}, bf16[16,1024]{1,0:T(8,128)(2,1)S(1)}) custom-call(bf16[128,1024]{1,0:T(8,128)(2,1)} %bitcast.6, bf16[128,1024]{1,0:T(8,128)(2,1)} %bitcast.7, bf16[128,1024]{1,0:T(8,128)(2,1)} %filt_hbm.1, bf16[128,1024]{1,0:T(8,128)(2,1)} %bitcast.8, ...), custom_call_target="tpu_custom_call" | custom-call | tf_op jit(solution)/shard_map/pallas_call | solution.py:367
  42.3 0.9 %shard_map.130 = (bf16[128,1024]{1,0:T(8,128)(2,1)}, bf16[128,1024]{1,0:T(8,128)(2,1)}, bf16[128,1024]{1,0:T(8,128)(2,1)}, bf16[16,1024]{1,0:T(8,128)(2,1)}) custom-call(bf16[128,1024]{1,0:T(8,128)(2,1)S(1)} %get-tuple-element.12.refs_0_, bf16[128,1024]{1,0:T(8,128)(2,1)S(1)} %get-tuple-element.13.refs_1_, bf16[128,1024]{1,0:T(8,128)(2,1)S(1)} %get-tuple-element.14.refs_2_, ...), custom_call_target="tpu_custom_call" | custom-call | tf_op jit(solution)/shard_map/pallas_call | solution.py:410

commit v4 on v3

--- a/solution.py
+++ b/solution.py
@@ -73,6 +73,7 @@
     out_buf,
     in_buf,
     in_filt,
+    out_part,
     in_part,
     out_sum,
     in_sum,
@@ -115,6 +116,11 @@
         )
     ]
 
+    def group_of(device):
+        return lax.rem(device, 2) * (ctx_size // 2) + device // 2
+
+    mine = group_of(me)
+
     barrier = pltpu.get_barrier_semaphore()
 
     def greet_ctx(step, carry):
@@ -150,13 +156,27 @@
         ).start()
 
     def exchange(which):
-        def send(step, carry):
-            peer = lax.rem(me + step, ctx_size)
-            remote(out_buf.at[which, peer], in_buf.at[which, me], which, (row, peer))
-            return carry
-
-        lax.fori_loop(1, ctx_size, send, 0)
-        in_buf[which, me] = out_buf[which, me]
+        for apart in (2, 1, 3, 0):
+            low = lax.rem(my_low + apart, share // 2)
+
+            def send(step, carry, low=low):
+                far_y = lax.rem(my_y + 2 + step // 2, lanes_x)
+                peer = far_y * share + low * 2 + lax.rem(me + step, 2)
+                leaving, landing = (group_of(peer), me) if which in (SIG, MID) else (peer, mine)
+                remote(
+                    out_buf.at[which, leaving], in_buf.at[which, landing], which, (row, peer)
+                )
+                return carry
+
+            if apart:
+                lax.fori_loop(0, share, send, 0)
+            else:
+                lax.fori_loop(0, share // 2, send, 0)
+                lax.fori_loop(share // 2 + 1, share, send, 0)
+        if which in (SIG, MID):
+            in_buf[which, me] = out_buf[which, mine]
+        else:
+            in_buf[which, mine] = out_buf[which, me]
 
     def wait_for(sem, which, count):
         part = in_buf.at[0, pl.ds(0, count)]
@@ -218,36 +238,48 @@
             values[:, own * LANES : (own + 1) * LANES].reshape(ctx_size, UNITS, LANES)
             for own in range(OWN)
         ]
-        out_buf[which] = jnp.concatenate(parts, axis=1).astype(BF16)
-
-    fetches = lax.rem(my_y + my_low, lanes_x) == my_x
+        message = jnp.concatenate(parts, axis=1).astype(BF16)
+        if which != GRF:
+            out_buf[which] = message
+            return
+        for pair in range(ctx_size // 2):
+            part_y, part_low = pair // (share // 2), pair % (share // 2)
+            group = (part_y + part_low) % lanes_x
+            out_part[group, 2 * part_y : 2 * part_y + 2] = message[2 * pair : 2 * pair + 2]
+
+    diagonal = my_y + my_low
     filt_slot = 2 * my_y + lax.rem(me, 2)
+    fetches_own = lax.rem(2 * diagonal, lanes_x) == my_x
 
     loads[0].wait()
-
-    @pl.when(fetches)
-    def _():
-        split_channels(FIL, lambda lanes: filt[:, lanes].astype(F32))
-
+    split_channels(FIL, lambda lanes: filt[:, lanes].astype(F32))
     loads[1].wait()
     split_channels(SIG, lambda lanes: signal[:, lanes].astype(F32))
     pl.semaphore_wait(barrier, ctx_size - 1 + lanes_x)
 
-    @pl.when(fetches)
+    def send_filter(step, carry):
+        far_y = lax.rem(my_y + 2 + step // 2, lanes_x)
+        low = lax.rem(my_x + 3 * lanes_x - diagonal - far_y, lanes_x)
+        peer = far_y * share + low * 2 + lax.rem(me + step, 2)
+
+        @pl.when(peer != me)
+        def _():
+            leaving = out_buf.at[FIL, group_of(peer)]
+            remote(leaving, in_filt.at[my_x, filt_slot], FIL, (row, peer))
+
+        return carry
+
+    lax.fori_loop(0, share, send_filter, 0)
+
+    @pl.when(fetches_own)
     def _():
-        def send(step, carry):
-            peer = lax.rem(me + step, ctx_size)
-            remote(out_buf.at[FIL, peer], in_filt.at[my_x, filt_slot], FIL, (row, peer))
-            return carry
-
-        lax.fori_loop(1, ctx_size, send, 0)
-        in_filt[my_x, filt_slot] = out_buf[FIL, me]
+        in_filt[my_x, filt_slot] = out_buf[FIL, mine]
 
     exchange(SIG)
     loads[2].wait()
     loads[3].wait()
     split_channels(MID, lambda lanes: gate[:, lanes].astype(F32) * cot[:, lanes].astype(F32))
-    wait_either(recv_sem, FIL, share, fetches)
+    wait_either(recv_sem, FIL, share, fetches_own)
     for step in range(1, lanes_x):
         peer = lax.rem(my_x + step, lanes_x) * 2 + my_z
         remote(in_filt.at[my_x], in_filt.at[my_x], FIL_X, (peer, me))
@@ -261,7 +293,7 @@
     wait_for(recv_sem, FIL_X, share * (lanes_x - 1))
     for pair in range(ctx_size // 2):
         part_y, part_low = pair // (share // 2), pair % (share // 2)
-        group = (part_y + part_low) % lanes_x
+        group = lax.rem(part_y + part_low + diagonal, lanes_x)
         line_up(in_filt[group, 2 * part_y : 2 * part_y + 2], 2 * pair, 2)
     transform(spec_h)
     multiply(spec_h, spec_x, False)
@@ -275,9 +307,8 @@
     transform_back(GRF)
     for step in range(1, lanes_x):
         peer = lax.rem(my_x + step, lanes_x)
-        blocks = out_buf.at[GRF, pl.ds(peer * share, share)]
-        remote(blocks, in_part.at[my_x], GRF_X, (peer * 2 + my_z, me))
-    in_part[my_x] = out_buf[GRF, pl.ds(my_x * share, share)]
+        remote(out_part.at[peer], in_part.at[my_x], GRF_X, (peer * 2 + my_z, me))
+    in_part[my_x] = out_part[my_x]
 
     multiply(spec_h, spec_g, True)
     transform_back(GRS)
@@ -288,12 +319,14 @@
     for part in range(1, lanes_x):
         total = total + in_part[part].astype(F32)
     out_sum[...] = total.astype(BF16)
-    to_row = me // per_row
-    slot = my_z * per_row + lax.rem(me, per_row)
-    stays = jnp.logical_and(to_row == row, me // share == my_x)
+    to_row = mine // per_row
+    slot = my_z * per_row + lax.rem(mine, per_row)
+    stays = jnp.logical_and(to_row == row, lax.rem(diagonal, lanes_x) == my_x)
 
     def send_sum(block, carry):
-        peer = my_x * share + block
+        far_y = block // 2
+        low = lax.rem(my_x + lanes_x - far_y, lanes_x)
+        peer = far_y * share + low * 2 + lax.rem(block, 2)
         leaves = jnp.logical_or(to_row != row, peer != me)
 
         @pl.when(leaves)
@@ -306,7 +339,7 @@
 
     @pl.when(stays)
     def _():
-        in_sum[slot] = out_sum[lax.rem(me, share)]
+        in_sum[slot] = out_sum[filt_slot]
 
     wait_for(recv_sem, CNV, ctx_size - 1)
     stage[...] = in_buf[CNV].astype(F32).reshape(ctx_size * OWN * UNITS, LANES)
@@ -334,10 +367,7 @@
     for which in (FIL_X, GRF_X):
         wait_for(send_sem, which, share * (lanes_x - 1))
     wait_either(send_sem, GRF, share, stays)
-
-    @pl.when(fetches)
-    def _():
-        wait_for(send_sem, FIL, ctx_size - 1)
+    wait_either(send_sem, FIL, share, fetches_own)
 
 
 def hand_on(*refs):
@@ -380,8 +410,9 @@
             pltpu.VMEM((2 * LANES, 2 * LANES), BF16),
             pltpu.VMEM((ROWS, LANES), F32),
             pltpu.VMEM((ROWS, LANES), F32),
-            pltpu.VMEM((6, ctx_size) + message, BF16),
+            pltpu.VMEM((5, ctx_size) + message, BF16),
             pltpu.VMEM((4, ctx_size) + message, BF16),
+            pltpu.VMEM((lanes_x, share) + message, BF16),
             pltpu.VMEM((lanes_x, share) + message, BF16),
             pltpu.VMEM((lanes_x, share) + message, BF16),
             pltpu.VMEM((share,) + message, BF16),

time: 43.9 us -> 42.8 us (0.975)
  Pallas kernels: 42.6 us -> 41.8 us
    pallas_call x1, Pallas kernels: 41.7 us -> 40.9 us  [per_device(): pl.pallas_call(functools.partial(kernel, ctx_size, dp_size), out_shape=tu...]
where the time goes in v4:
time: 42.8 us; the launch traced here: 42.4 us
  Pallas kernels  41.8 us (98%)
  between operations  0.64 us (1%)
    pallas_call x1, Pallas kernels, per_device(): pl.pallas_call(functools.partial(kernel, ctx_size, dp_size), out_shape=tu...  40.9 us
    pallas_call x1, Pallas kernels, per_device(): pl.pallas_call(hand_on, out_shape=tuple((jax.ShapeDtypeStruct(shape, BF16...  0.91 us

profile of v4, /device:TPU:1, one launch (start us, length us, event | category | flops | bytes accessed | tf_op | source)
XLA Modules:
  0.0 42.4 jit_solution(11063621078471687601)
XLA Ops:
  0.6 40.9 %shard_map.129 = (bf16[128,1024]{1,0:T(8,128)(2,1)S(1)}, bf16[128,1024]{1,0:T(8,128)(2,1)S(1)}, bf16[128,1024]{1,0:T(8,128)(2,1)S(1)}, bf16[16,1024]{1,0:T(8,128)(2,1)S(1)}) custom-call(bf16[128,1024]{1,0:T(8,128)(2,1)} %bitcast.6, bf16[128,1024]{1,0:T(8,128)(2,1)} %bitcast.7, bf16[128,1024]{1,0:T(8,128)(2,1)} %filt_hbm.1, bf16[128,1024]{1,0:T(8,128)(2,1)} %bitcast.8, ...), custom_call_target="tpu_custom_call" | custom-call | tf_op jit(solution)/shard_map/pallas_call | solution.py:397
  41.5 0.9 %shard_map.130 = (bf16[128,1024]{1,0:T(8,128)(2,1)}, bf16[128,1024]{1,0:T(8,128)(2,1)}, bf16[128,1024]{1,0:T(8,128)(2,1)}, bf16[16,1024]{1,0:T(8,128)(2,1)}) custom-call(bf16[128,1024]{1,0:T(8,128)(2,1)S(1)} %get-tuple-element.12.refs_0_, bf16[128,1024]{1,0:T(8,128)(2,1)S(1)} %get-tuple-element.13.refs_1_, bf16[128,1024]{1,0:T(8,128)(2,1)S(1)} %get-tuple-element.14.refs_2_, ...), custom_call_target="tpu_custom_call" | custom-call | tf_op jit(solution)/shard_map/pallas_call | solution.py:441

commit v5 on v4

--- a/solution.py
+++ b/solution.py
@@ -116,8 +116,11 @@
         )
     ]
 
+    for copy in loads[0:2]:
+        copy.start()
+
     def group_of(device):
-        return lax.rem(device, 2) * (ctx_size // 2) + device // 2
+        return 16 * (lax.rem(device, 2)) + 8 * (lax.rem(device // 4, 2)) + 4 * (lax.rem(device // 2, 2)) + 2 * (device // 16) + 1 * (lax.rem(device // 8, 2))
 
     mine = group_of(me)
 
@@ -135,7 +138,7 @@
     other = my_x * 2 + 1 - my_z
     pl.semaphore_signal(barrier, inc=1, device_id=(other, me), device_id_type=MESH)
 
-    for copy in loads:
+    for copy in loads[2:]:
         copy.start()
 
     def split_channels(which, block):
@@ -253,8 +256,6 @@
 
     loads[0].wait()
     split_channels(FIL, lambda lanes: filt[:, lanes].astype(F32))
-    loads[1].wait()
-    split_channels(SIG, lambda lanes: signal[:, lanes].astype(F32))
     pl.semaphore_wait(barrier, ctx_size - 1 + lanes_x)
 
     def send_filter(step, carry):
@@ -275,6 +276,8 @@
     def _():
         in_filt[my_x, filt_slot] = out_buf[FIL, mine]
 
+    loads[1].wait()
+    split_channels(SIG, lambda lanes: signal[:, lanes].astype(F32))
     exchange(SIG)
     loads[2].wait()
     loads[3].wait()
@@ -305,37 +308,44 @@
     transform(spec_g)
     multiply(spec_x, spec_g, True)
     transform_back(GRF)
-    for step in range(1, lanes_x):
-        peer = lax.rem(my_x + step, lanes_x)
-        remote(out_part.at[peer], in_part.at[my_x], GRF_X, (peer * 2 + my_z, me))
+    for part_y in range(lanes_x):
+        for step in range(1, lanes_x):
+            peer = lax.rem(my_x + step, lanes_x)
+            blocks = pl.ds(2 * part_y, 2)
+            remote(
+                out_part.at[peer, blocks],
+                in_part.at[my_x, blocks],
+                GRF_X + part_y,
+                (peer * 2 + my_z, me),
+            )
     in_part[my_x] = out_part[my_x]
 
     multiply(spec_h, spec_g, True)
     transform_back(GRS)
     exchange(GRS)
 
-    wait_for(recv_sem, GRF_X, share * (lanes_x - 1))
-    total = in_part[0].astype(F32)
-    for part in range(1, lanes_x):
-        total = total + in_part[part].astype(F32)
-    out_sum[...] = total.astype(BF16)
     to_row = mine // per_row
     slot = my_z * per_row + lax.rem(mine, per_row)
     stays = jnp.logical_and(to_row == row, lax.rem(diagonal, lanes_x) == my_x)
 
-    def send_sum(block, carry):
-        far_y = block // 2
-        low = lax.rem(my_x + lanes_x - far_y, lanes_x)
-        peer = far_y * share + low * 2 + lax.rem(block, 2)
-        leaves = jnp.logical_or(to_row != row, peer != me)
-
-        @pl.when(leaves)
-        def _():
-            remote(out_sum.at[block], in_sum.at[slot], GRF, (to_row, peer))
-
-        return carry
-
-    lax.fori_loop(0, share, send_sum, 0)
+    def send_sums(part_y):
+        wait_for(recv_sem, GRF_X + part_y, 2 * (lanes_x - 1))
+        blocks = slice(2 * part_y, 2 * part_y + 2)
+        total = in_part[0, blocks].astype(F32)
+        for part in range(1, lanes_x):
+            total = total + in_part[part, blocks].astype(F32)
+        out_sum[blocks] = total.astype(BF16)
+        low = lax.rem(my_x + lanes_x - part_y, lanes_x)
+        for block in (2 * part_y, 2 * part_y + 1):
+            peer = part_y * share + low * 2 + block % 2
+            leaves = jnp.logical_or(to_row != row, peer != me)
+
+            @pl.when(leaves)
+            def _(block=block, peer=peer):
+                remote(out_sum.at[block], in_sum.at[slot], GRF, (to_row, peer))
+
+    for part_y in range(lanes_x):
+        send_sums(part_y)
 
     @pl.when(stays)
     def _():
@@ -364,8 +374,9 @@
 
     for which in (SIG, MID, CNV, GRS):
         wait_for(send_sem, which, ctx_size - 1)
-    for which in (FIL_X, GRF_X):
-        wait_for(send_sem, which, share * (lanes_x - 1))
+    wait_for(send_sem, FIL_X, share * (lanes_x - 1))
+    for part_y in range(lanes_x):
+        wait_for(send_sem, GRF_X + part_y, 2 * (lanes_x - 1))
     wait_either(send_sem, GRF, share, stays)
     wait_either(send_sem, FIL, share, fetches_own)
 
@@ -424,8 +435,8 @@
             spectrum,
             spectrum,
             spectrum,
-            pltpu.SemaphoreType.DMA((8,)),
-            pltpu.SemaphoreType.DMA((8,)),
+            pltpu.SemaphoreType.DMA((7 + lanes_x,)),
+            pltpu.SemaphoreType.DMA((7 + lanes_x,)),
             pltpu.SemaphoreType.DMA((10,)),
         ],
         compiler_params=pltpu.CompilerParams(

time: 42.8 us -> 41.8 us (0.977)
  the two profiles are of different devices: /device:TPU:1 before, /device:TPU:25 now
where the time goes in v5:
time: 41.8 us; the launch traced here: 41.7 us
  Pallas kernels  41 us (98%)
  between operations  0.64 us (2%)
    pallas_call x1, Pallas kernels, per_device(): pl.pallas_call(functools.partial(kernel, ctx_size, dp_size), out_shape=tu...  40.1 us
    pallas_call x1, Pallas kernels, per_device(): pl.pallas_call(hand_on, out_shape=tuple((jax.ShapeDtypeStruct(shape, BF16...  0.91 us

profile of v5, /device:TPU:25, one launch (start us, length us, event | category | flops | bytes accessed | tf_op | source)
XLA Modules:
  0.0 41.7 jit_solution(3014316821212880460)
XLA Ops:
  0.6 40.1 %shard_map.129 = (bf16[128,1024]{1,0:T(8,128)(2,1)S(1)}, bf16[128,1024]{1,0:T(8,128)(2,1)S(1)}, bf16[128,1024]{1,0:T(8,128)(2,1)S(1)}, bf16[16,1024]{1,0:T(8,128)(2,1)S(1)}) custom-call(bf16[128,1024]{1,0:T(8,128)(2,1)} %bitcast.6, bf16[128,1024]{1,0:T(8,128)(2,1)} %bitcast.7, bf16[128,1024]{1,0:T(8,128)(2,1)} %filt_hbm.1, bf16[128,1024]{1,0:T(8,128)(2,1)} %bitcast.8, ...), custom_call_target="tpu_custom_call" | custom-call | tf_op jit(solution)/shard_map/pallas_call | solution.py:408
  40.7 0.9 %shard_map.130 = (bf16[128,1024]{1,0:T(8,128)(2,1)}, bf16[128,1024]{1,0:T(8,128)(2,1)}, bf16[128,1024]{1,0:T(8,128)(2,1)}, bf16[16,1024]{1,0:T(8,128)(2,1)}) custom-call(bf16[128,1024]{1,0:T(8,128)(2,1)S(1)} %get-tuple-element.12.refs_0_, bf16[128,1024]{1,0:T(8,128)(2,1)S(1)} %get-tuple-element.13.refs_1_, bf16[128,1024]{1,0:T(8,128)(2,1)S(1)} %get-tuple-element.14.refs_2_, ...), custom_call_target="tpu_custom_call" | custom-call | tf_op jit(solution)/shard_map/pallas_call | solution.py:452

commit v6 on v5

--- a/solution.py
+++ b/solution.py
@@ -120,7 +120,7 @@
         copy.start()
 
     def group_of(device):
-        return 16 * (lax.rem(device, 2)) + 8 * (lax.rem(device // 4, 2)) + 4 * (lax.rem(device // 2, 2)) + 2 * (device // 16) + 1 * (lax.rem(device // 8, 2))
+        return 16 * (lax.rem(device, 2)) + 8 * (lax.rem(device // 8, 2)) + 4 * (lax.rem(device // 2, 2)) + 2 * (device // 16) + 1 * (lax.rem(device // 4, 2))
 
     mine = group_of(me)
 
@@ -308,7 +308,8 @@
     transform(spec_g)
     multiply(spec_x, spec_g, True)
     transform_back(GRF)
-    for part_y in range(lanes_x):
+    for turn in range(lanes_x):
+        part_y = lax.rem(my_y + 2 + turn, lanes_x)
         for step in range(1, lanes_x):
             peer = lax.rem(my_x + step, lanes_x)
             blocks = pl.ds(2 * part_y, 2)
@@ -330,22 +331,23 @@
 
     def send_sums(part_y):
         wait_for(recv_sem, GRF_X + part_y, 2 * (lanes_x - 1))
-        blocks = slice(2 * part_y, 2 * part_y + 2)
+        blocks = pl.ds(2 * part_y, 2)
         total = in_part[0, blocks].astype(F32)
         for part in range(1, lanes_x):
             total = total + in_part[part, blocks].astype(F32)
         out_sum[blocks] = total.astype(BF16)
         low = lax.rem(my_x + lanes_x - part_y, lanes_x)
-        for block in (2 * part_y, 2 * part_y + 1):
-            peer = part_y * share + low * 2 + block % 2
+        for core in range(2):
+            block = 2 * part_y + core
+            peer = part_y * share + low * 2 + core
             leaves = jnp.logical_or(to_row != row, peer != me)
 
             @pl.when(leaves)
             def _(block=block, peer=peer):
                 remote(out_sum.at[block], in_sum.at[slot], GRF, (to_row, peer))
 
-    for part_y in range(lanes_x):
-        send_sums(part_y)
+    for turn in range(lanes_x):
+        send_sums(lax.rem(my_y + 2 + turn, lanes_x))
 
     @pl.when(stays)
     def _():

time: 41.8 us -> 41.1 us (0.983)
  the two profiles are of different devices: /device:TPU:25 before, /device:TPU:1 now
where the time goes in v6:
time: 41.1 us; the launch traced here: 41 us
  Pallas kernels  40.4 us (98%)
  between operations  0.64 us (2%)
    pallas_call x1, Pallas kernels, per_device(): pl.pallas_call(functools.partial(kernel, ctx_size, dp_size), out_shape=tu...  39.5 us
    pallas_call x1, Pallas kernels, per_device(): pl.pallas_call(hand_on, out_shape=tuple((jax.ShapeDtypeStruct(shape, BF16...  0.91 us

profile of v6, /device:TPU:1, one launch (start us, length us, event | category | flops | bytes accessed | tf_op | source)
XLA Modules:
  0.0 41.0 jit_solution(12858285098844017761)
XLA Ops:
  0.6 39.5 %shard_map.129 = (bf16[128,1024]{1,0:T(8,128)(2,1)S(1)}, bf16[128,1024]{1,0:T(8,128)(2,1)S(1)}, bf16[128,1024]{1,0:T(8,128)(2,1)S(1)}, bf16[16,1024]{1,0:T(8,128)(2,1)S(1)}) custom-call(bf16[128,1024]{1,0:T(8,128)(2,1)} %bitcast.6, bf16[128,1024]{1,0:T(8,128)(2,1)} %bitcast.7, bf16[128,1024]{1,0:T(8,128)(2,1)} %filt_hbm.1, bf16[128,1024]{1,0:T(8,128)(2,1)} %bitcast.8, ...), custom_call_target="tpu_custom_call" | custom-call | tf_op jit(solution)/shard_map/pallas_call | solution.py:410
  40.1 0.9 %shard_map.130 = (bf16[128,1024]{1,0:T(8,128)(2,1)}, bf16[128,1024]{1,0:T(8,128)(2,1)}, bf16[128,1024]{1,0:T(8,128)(2,1)}, bf16[16,1024]{1,0:T(8,128)(2,1)}) custom-call(bf16[128,1024]{1,0:T(8,128)(2,1)S(1)} %get-tuple-element.12.refs_0_, bf16[128,1024]{1,0:T(8,128)(2,1)S(1)} %get-tuple-element.13.refs_1_, bf16[128,1024]{1,0:T(8,128)(2,1)S(1)} %get-tuple-element.14.refs_2_, ...), custom_call_target="tpu_custom_call" | custom-call | tf_op jit(solution)/shard_map/pallas_call | solution.py:454
